TPU v7x, 512 devices: a whole 4x8x8 slice. The times are simulated.
512 devices in a mesh: bucket: 16 (over z, core), ref: 32 (over x, y).
Axes of the slice: x: 4, y: 8, z: 8, core: 2. Of those that a mesh axis runs over, the one named last changes fastest.
Arguments:
- gen_points: bfloat16 [68, 49152], P(None, 'bucket'), may hold values from -6 to 6
- bucket_id: int32 [49152], P('bucket'), may hold values from 0 to 15, as said below
- ref_points: bfloat16 [16384, 68, 128], P(('bucket', 'ref')), may hold values from -6 to 6
- block_pairs: int32 [16, 32, 2, 768], P('bucket', 'ref'), may hold values from 0 to 31, as said below
- pair_count: int32 [16, 32], P('bucket', 'ref'), may hold values from 32 to 768, as said below
Outputs:
- gen_dist: float32 [49152], P('bucket')
- ref_dist: float32 [16384, 128], P(('bucket', 'ref'))
Inputs may be any that keep to these rules, and one draw needn't show every extreme that they name: `bucket_id`: every source sends between 129 and 256 of its 3072 points to every bucket; in every draw some bucket receives exactly 256 points from every source. `block_pairs`: row 0 holds numbers below 32, row 1 numbers below 32. Among the live pairs of a device every one of its reference blocks is named, and every generated block of a bucket is named by a live pair on some shard of that bucket. `pair_count`: some device's list is full in every draw.
All inputs are finite; a program needn't handle non-finite values.
Results may differ from a plain program's by a relative error of at most 0.0003.
Values may be sent and summed in bfloat16 or wider, within the bound.
A program may use at most 64 MiB of HBM per device.

v0:
```python
import math

import jax
import jax.numpy as jnp
from jax import lax
from jax.sharding import PartitionSpec as P

BLK = 128


def tile_minima(gen_blocks, gen_norm, gen_live, ref_blocks, ref_norm, pair_list, live_count):
    pair_total = pair_list.shape[1]
    step_len = math.gcd(pair_total, 64)
    gen_count = gen_blocks.shape[0]
    ref_count = ref_blocks.shape[0]
    channels = gen_blocks.shape[1]
    block_len = gen_blocks.shape[2]
    gen_ids = jnp.arange(gen_count, dtype=jnp.int32)
    ref_ids = jnp.arange(ref_count, dtype=jnp.int32)

    def advance(state_pair, offset):
        row_min, col_min = state_pair
        gen_pick = lax.dynamic_slice_in_dim(pair_list[0], offset, step_len)
        ref_pick = lax.dynamic_slice_in_dim(pair_list[1], offset, step_len)
        active = offset + jnp.arange(step_len, dtype=jnp.int32) < live_count
        gen_tiles = gen_blocks[gen_pick]
        ref_tiles = ref_blocks[ref_pick]
        products = jnp.einsum(
            "pfi,pfj->pij", gen_tiles, ref_tiles, preferred_element_type=jnp.float32
        )
        distance = (
            gen_norm[gen_pick][:, :, None] + ref_norm[ref_pick][:, None, :] - 2.0 * products
        ) / channels
        row_part = jnp.min(jnp.where(active[:, None, None], distance, jnp.inf), axis=2)
        col_ok = active[:, None, None] & (gen_live[gen_pick][:, :, None] > 0)
        col_part = jnp.min(jnp.where(col_ok, distance, jnp.inf), axis=1)
        row_hit = gen_pick[None, :] == gen_ids[:, None]
        row_min = jnp.minimum(
            row_min, jnp.min(jnp.where(row_hit[:, :, None], row_part[None], jnp.inf), axis=1)
        )
        col_hit = ref_pick[None, :] == ref_ids[:, None]
        col_min = jnp.minimum(
            col_min, jnp.min(jnp.where(col_hit[:, :, None], col_part[None], jnp.inf), axis=1)
        )
        return ((row_min, col_min), None)

    offsets = jnp.arange(0, pair_total, step_len, dtype=jnp.int32)
    initial = (
        jnp.full((gen_count, block_len), jnp.inf, jnp.float32),
        jnp.full((ref_count, block_len), jnp.inf, jnp.float32),
    )
    (row_min, col_min), ignored = lax.scan(advance, initial, offsets)
    return (row_min, col_min)


def per_device(gen_points, bucket_id, ref_points, block_pairs, pair_count):
    owners = lax.axis_size("bucket")
    channels = gen_points.shape[0]
    owner_ids = jnp.arange(owners, dtype=jnp.int32)
    matches = (bucket_id[None, :] == owner_ids[:, None]).astype(jnp.int32)
    earlier = jnp.cumsum(matches, axis=1) - matches
    slot_rank = jnp.sum(earlier * matches, axis=0)
    dest_block = 2 * bucket_id + slot_rank // BLK
    slot_offset = slot_rank % BLK
    outgoing = (
        jnp.zeros((2 * owners, channels, BLK), jnp.bfloat16)
        .at[dest_block, :, slot_offset]
        .set(gen_points.T)
    )
    live_flags = (
        jnp.zeros((2 * owners, 1, BLK), jnp.bfloat16)
        .at[dest_block, 0, slot_offset]
        .set(jnp.bfloat16(1))
    )
    incoming, incoming_live = (
        lax.all_to_all(outgoing, "bucket", split_axis=0, concat_axis=0, tiled=True),
        lax.all_to_all(live_flags, "bucket", split_axis=0, concat_axis=0, tiled=True),
    )
    gen_live = (incoming_live[:, 0, :] > 0.5).astype(jnp.int32)
    gen_norm = jnp.einsum("bfi,bfi->bi", incoming, incoming, preferred_element_type=jnp.float32)
    ref_norm = jnp.einsum("bfi,bfi->bi", ref_points, ref_points, preferred_element_type=jnp.float32)
    row_min, col_min = tile_minima(
        incoming, gen_norm, gen_live, ref_points, ref_norm, block_pairs[0, 0], pair_count[0, 0]
    )
    merged = lax.pmin(row_min, "ref")
    back_rows = lax.all_to_all(merged, "bucket", split_axis=0, concat_axis=0, tiled=True)
    gen_dist = back_rows[dest_block, slot_offset]
    return (gen_dist, col_min)


def solution(mesh):
    placed = (
        P(None, "bucket"),
        P("bucket"),
        P(("bucket", "ref"), None, None),
        P("bucket", "ref", None, None),
        P("bucket", "ref"),
    )
    return jax.shard_map(
        per_device,
        mesh=mesh,
        in_specs=placed,
        out_specs=(P("bucket"), P(("bucket", "ref"), None)),
        check_vma=False,
    )
```

profile of v0, /device:TPU:1, one launch (start us, length us, event | category | flops | bytes accessed | tf_op | source)
XLA Modules:
  0.0 450.2 jit_solution(17832285990143225760)
XLA Ops:
  1.5 4.6 %reduce-window.6 = s32[16,24,128]{2,1,0:T(8,128)S(1)} reduce-window(s32[16,24,128]{2,1,0:T(8,128)S(1)} %fusion.10, s32[]{:T(128)} %constant.67.clone.1), window={size=1x1x128 pad=0_0x0_0x127_0}, to_apply=%region_0.0 | reduce-window | flops 6242304 | bytes 393220 | tf_op jit(solution)/shard_map/reduce-window
  6.7 0.8 select_reduce_fusion.4
  9.3 21.6 %scatter_custom_fusion.1 = bf16[4096]{0:T(1024)(128)(2,1)S(1)} fusion(s32[3072]{0:T(1024)S(1)} %broadcast_select_fusion, bf16[3072]{0:T(1024)(128)(2,1)S(1)} %broadcast.248, bf16[]{:T(256)} %constant.70.clone.1), kind=kCustom, calls=%fused_computation.66 | custom fusion | bytes 8194
  31.5 11.8 %all-to-all-start.1 = ((bf16[16,2,128]{2,1,0:T(2,128)(2,1)}), bf16[16,2,128]{2,1,0:T(2,128)(2,1)S(1)}, u32[]{:S(2)}, u32[]{:S(2)}) async-start(bf16[16,2,128]{2,1,0:T(2,128)(2,1)} %bitcast.51), calls=%async_computation.1 | async-start | bytes 16384 | tf_op jit(solution)/shard_map/all_to_all | solution.py:77
  44.0 8.6 %scatter_custom_fusion = bf16[68,4096]{0,1:T(8,128)(2,1)S(1)} fusion(s32[3072]{0:T(1024)S(1)} %broadcast_select_fusion.1, bf16[3072,68]{1,0:T(8,128)(2,1)S(1)} %copy.20, bf16[]{:T(256)} %constant.70.clone.1), kind=kCustom, calls=%fused_computation.34 | custom fusion | bytes 557058
  52.6 1.3 copy.21
  53.9 7.2 %all-to-all-start = ((bf16[32,68,128]{2,1,0:T(8,128)(2,1)}), bf16[32,68,128]{2,1,0:T(8,128)(2,1)S(1)}, u32[]{:S(2)}, u32[]{:S(2)}) async-start(bf16[32,68,128]{2,1,0:T(8,128)(2,1)} %bitcast.12), calls=%async_computation | async-start | bytes 1179648 | tf_op jit(solution)/shard_map/all_to_all | solution.py:76
  61.6 18.2 %all-to-all-done = bf16[32,68,128]{2,1,0:T(8,128)(2,1)S(1)} async-done(((bf16[32,68,128]{2,1,0:T(8,128)(2,1)}), bf16[32,68,128]{2,1,0:T(8,128)(2,1)S(1)}, u32[]{:S(2)}, u32[]{:S(2)}) %all-to-all-start) | async-done | bytes 557088 | tf_op jit(solution)/shard_map/all_to_all | solution.py:76
  79.9 184.3 %while.15 = (s32[]{:T(128)}, f32[32,128]{1,0:T(8,128)S(1)}, f32[32,128]{1,0:T(8,128)S(1)}, s32[2,768]{1,0:T(2,128)S(1)}, s32[12]{0:T(128)S(1)}, /*index=5*/s32[]...) while((s32[]{:T(128)}, f32[32,128]{1,0:T(8,128)S(1)}, ...), condition=%wide.region_10.11_spmd.clone.clone, body=%wide.region_5.10_spmd.clone.clone.sunk | while | flops 152058368 | bytes 7291541 | solution.py:52
  83.2 1.3 add_compare_fusion.2
  86.0 1.7 gather_fusion.4
  88.4 6.0 %select_reduce_fusion.8 = (f32[64,128]{1,0:T(8,128)S(1)}, f32[64,128]{1,0:T(8,128)S(1)}) fusion(f32[64,128]{1,0:T(8,128)S(1)} %gather_fusion, f32[64,128]{1,0:T(8,128)S(1)} %gather_fusion.1, pred[64,128]{1,0:T(8,128)(4,1)S(1)} %compare_and_fusion.2, pred[64]{0:T(512)(128)(4,1)S(1)} %add_compare_fusion.2, bf16[64,68,128]{2,1,0:T(8,128)(2,1)S(1)} %gather_fusion.3, ...), kind=kOutput, calls=%fused_computation.9.clone.1 | convolution fusion | flops 150978560 | bytes 2367552 | tf_op jit(solution)/shard_map/while/body/eval_jaxpr/pfi,pfj->pij/dot_general | solution.py:28
  98.5 1.3 add_compare_fusion.2
  101.4 1.7 gather_fusion.4
  103.7 6.0 %select_reduce_fusion.8 = (f32[64,128]{1,0:T(8,128)S(1)}, f32[64,128]{1,0:T(8,128)S(1)}) fusion(f32[64,128]{1,0:T(8,128)S(1)} %gather_fusion, f32[64,128]{1,0:T(8,128)S(1)} %gather_fusion.1, pred[64,128]{1,0:T(8,128)(4,1)S(1)} %compare_and_fusion.2, pred[64]{0:T(512)(128)(4,1)S(1)} %add_compare_fusion.2, bf16[64,68,128]{2,1,0:T(8,128)(2,1)S(1)} %gather_fusion.3, ...), kind=kOutput, calls=%fused_computation.9.clone.1 | convolution fusion | flops 150978560 | bytes 2367552 | tf_op jit(solution)/shard_map/while/body/eval_jaxpr/pfi,pfj->pij/dot_general | solution.py:28
  113.9 1.3 add_compare_fusion.2
  116.7 1.7 gather_fusion.4
  119.1 6.0 %select_reduce_fusion.8 = (f32[64,128]{1,0:T(8,128)S(1)}, f32[64,128]{1,0:T(8,128)S(1)}) fusion(f32[64,128]{1,0:T(8,128)S(1)} %gather_fusion, f32[64,128]{1,0:T(8,128)S(1)} %gather_fusion.1, pred[64,128]{1,0:T(8,128)(4,1)S(1)} %compare_and_fusion.2, pred[64]{0:T(512)(128)(4,1)S(1)} %add_compare_fusion.2, bf16[64,68,128]{2,1,0:T(8,128)(2,1)S(1)} %gather_fusion.3, ...), kind=kOutput, calls=%fused_computation.9.clone.1 | convolution fusion | flops 150978560 | bytes 2367552 | tf_op jit(solution)/shard_map/while/body/eval_jaxpr/pfi,pfj->pij/dot_general | solution.py:28
  129.2 1.3 add_compare_fusion.2
  132.1 1.7 gather_fusion.4
  134.4 6.0 %select_reduce_fusion.8 = (f32[64,128]{1,0:T(8,128)S(1)}, f32[64,128]{1,0:T(8,128)S(1)}) fusion(f32[64,128]{1,0:T(8,128)S(1)} %gather_fusion, f32[64,128]{1,0:T(8,128)S(1)} %gather_fusion.1, pred[64,128]{1,0:T(8,128)(4,1)S(1)} %compare_and_fusion.2, pred[64]{0:T(512)(128)(4,1)S(1)} %add_compare_fusion.2, bf16[64,68,128]{2,1,0:T(8,128)(2,1)S(1)} %gather_fusion.3, ...), kind=kOutput, calls=%fused_computation.9.clone.1 | convolution fusion | flops 150978560 | bytes 2367552 | tf_op jit(solution)/shard_map/while/body/eval_jaxpr/pfi,pfj->pij/dot_general | solution.py:28
  144.6 1.3 add_compare_fusion.2
  147.5 1.7 gather_fusion.4
  149.8 6.0 %select_reduce_fusion.8 = (f32[64,128]{1,0:T(8,128)S(1)}, f32[64,128]{1,0:T(8,128)S(1)}) fusion(f32[64,128]{1,0:T(8,128)S(1)} %gather_fusion, f32[64,128]{1,0:T(8,128)S(1)} %gather_fusion.1, pred[64,128]{1,0:T(8,128)(4,1)S(1)} %compare_and_fusion.2, pred[64]{0:T(512)(128)(4,1)S(1)} %add_compare_fusion.2, bf16[64,68,128]{2,1,0:T(8,128)(2,1)S(1)} %gather_fusion.3, ...), kind=kOutput, calls=%fused_computation.9.clone.1 | convolution fusion | flops 150978560 | bytes 2367552 | tf_op jit(solution)/shard_map/while/body/eval_jaxpr/pfi,pfj->pij/dot_general | solution.py:28
  160.0 1.3 add_compare_fusion.2
  162.8 1.7 gather_fusion.4
  165.1 6.0 %select_reduce_fusion.8 = (f32[64,128]{1,0:T(8,128)S(1)}, f32[64,128]{1,0:T(8,128)S(1)}) fusion(f32[64,128]{1,0:T(8,128)S(1)} %gather_fusion, f32[64,128]{1,0:T(8,128)S(1)} %gather_fusion.1, pred[64,128]{1,0:T(8,128)(4,1)S(1)} %compare_and_fusion.2, pred[64]{0:T(512)(128)(4,1)S(1)} %add_compare_fusion.2, bf16[64,68,128]{2,1,0:T(8,128)(2,1)S(1)} %gather_fusion.3, ...), kind=kOutput, calls=%fused_computation.9.clone.1 | convolution fusion | flops 150978560 | bytes 2367552 | tf_op jit(solution)/shard_map/while/body/eval_jaxpr/pfi,pfj->pij/dot_general | solution.py:28
  175.3 1.3 add_compare_fusion.2
  178.2 1.7 gather_fusion.4
  180.5 6.0 %select_reduce_fusion.8 = (f32[64,128]{1,0:T(8,128)S(1)}, f32[64,128]{1,0:T(8,128)S(1)}) fusion(f32[64,128]{1,0:T(8,128)S(1)} %gather_fusion, f32[64,128]{1,0:T(8,128)S(1)} %gather_fusion.1, pred[64,128]{1,0:T(8,128)(4,1)S(1)} %compare_and_fusion.2, pred[64]{0:T(512)(128)(4,1)S(1)} %add_compare_fusion.2, bf16[64,68,128]{2,1,0:T(8,128)(2,1)S(1)} %gather_fusion.3, ...), kind=kOutput, calls=%fused_computation.9.clone.1 | convolution fusion | flops 150978560 | bytes 2367552 | tf_op jit(solution)/shard_map/while/body/eval_jaxpr/pfi,pfj->pij/dot_general | solution.py:28
  190.7 1.3 add_compare_fusion.2
  193.5 1.7 gather_fusion.4
  195.8 6.0 %select_reduce_fusion.8 = (f32[64,128]{1,0:T(8,128)S(1)}, f32[64,128]{1,0:T(8,128)S(1)}) fusion(f32[64,128]{1,0:T(8,128)S(1)} %gather_fusion, f32[64,128]{1,0:T(8,128)S(1)} %gather_fusion.1, pred[64,128]{1,0:T(8,128)(4,1)S(1)} %compare_and_fusion.2, pred[64]{0:T(512)(128)(4,1)S(1)} %add_compare_fusion.2, bf16[64,68,128]{2,1,0:T(8,128)(2,1)S(1)} %gather_fusion.3, ...), kind=kOutput, calls=%fused_computation.9.clone.1 | convolution fusion | flops 150978560 | bytes 2367552 | tf_op jit(solution)/shard_map/while/body/eval_jaxpr/pfi,pfj->pij/dot_general | solution.py:28
  206.0 1.3 add_compare_fusion.2
  208.9 1.7 gather_fusion.4
  211.2 6.0 %select_reduce_fusion.8 = (f32[64,128]{1,0:T(8,128)S(1)}, f32[64,128]{1,0:T(8,128)S(1)}) fusion(f32[64,128]{1,0:T(8,128)S(1)} %gather_fusion, f32[64,128]{1,0:T(8,128)S(1)} %gather_fusion.1, pred[64,128]{1,0:T(8,128)(4,1)S(1)} %compare_and_fusion.2, pred[64]{0:T(512)(128)(4,1)S(1)} %add_compare_fusion.2, bf16[64,68,128]{2,1,0:T(8,128)(2,1)S(1)} %gather_fusion.3, ...), kind=kOutput, calls=%fused_computation.9.clone.1 | convolution fusion | flops 150978560 | bytes 2367552 | tf_op jit(solution)/shard_map/while/body/eval_jaxpr/pfi,pfj->pij/dot_general | solution.py:28
  221.4 1.3 add_compare_fusion.2
  224.2 1.7 gather_fusion.4
  226.6 6.0 %select_reduce_fusion.8 = (f32[64,128]{1,0:T(8,128)S(1)}, f32[64,128]{1,0:T(8,128)S(1)}) fusion(f32[64,128]{1,0:T(8,128)S(1)} %gather_fusion, f32[64,128]{1,0:T(8,128)S(1)} %gather_fusion.1, pred[64,128]{1,0:T(8,128)(4,1)S(1)} %compare_and_fusion.2, pred[64]{0:T(512)(128)(4,1)S(1)} %add_compare_fusion.2, bf16[64,68,128]{2,1,0:T(8,128)(2,1)S(1)} %gather_fusion.3, ...), kind=kOutput, calls=%fused_computation.9.clone.1 | convolution fusion | flops 150978560 | bytes 2367552 | tf_op jit(solution)/shard_map/while/body/eval_jaxpr/pfi,pfj->pij/dot_general | solution.py:28
  236.7 1.3 add_compare_fusion.2
  239.6 1.7 gather_fusion.4
  241.9 6.0 %select_reduce_fusion.8 = (f32[64,128]{1,0:T(8,128)S(1)}, f32[64,128]{1,0:T(8,128)S(1)}) fusion(f32[64,128]{1,0:T(8,128)S(1)} %gather_fusion, f32[64,128]{1,0:T(8,128)S(1)} %gather_fusion.1, pred[64,128]{1,0:T(8,128)(4,1)S(1)} %compare_and_fusion.2, pred[64]{0:T(512)(128)(4,1)S(1)} %add_compare_fusion.2, bf16[64,68,128]{2,1,0:T(8,128)(2,1)S(1)} %gather_fusion.3, ...), kind=kOutput, calls=%fused_computation.9.clone.1 | convolution fusion | flops 150978560 | bytes 2367552 | tf_op jit(solution)/shard_map/while/body/eval_jaxpr/pfi,pfj->pij/dot_general | solution.py:28
  252.1 1.3 add_compare_fusion.2
  255.0 1.7 gather_fusion.4
  257.3 6.0 %select_reduce_fusion.8 = (f32[64,128]{1,0:T(8,128)S(1)}, f32[64,128]{1,0:T(8,128)S(1)}) fusion(f32[64,128]{1,0:T(8,128)S(1)} %gather_fusion, f32[64,128]{1,0:T(8,128)S(1)} %gather_fusion.1, pred[64,128]{1,0:T(8,128)(4,1)S(1)} %compare_and_fusion.2, pred[64]{0:T(512)(128)(4,1)S(1)} %add_compare_fusion.2, bf16[64,68,128]{2,1,0:T(8,128)(2,1)S(1)} %gather_fusion.3, ...), kind=kOutput, calls=%fused_computation.9.clone.1 | convolution fusion | flops 150978560 | bytes 2367552 | tf_op jit(solution)/shard_map/while/body/eval_jaxpr/pfi,pfj->pij/dot_general | solution.py:28
  264.2 116.1 %pmin.7 = f32[16,2,128]{2,1,0:T(2,128)S(1)} all-reduce(f32[16,2,128]{2,1,0:T(2,128)S(1)} %bitcast.74), channel_id=1, replica_groups=mesh['bucket'=16,'ref'=32] {'ref'}, use_global_device_ids=true, to_apply=%region_11.12 | all-reduce | flops 4096 | bytes 32768 | tf_op jit(solution)/shard_map/pmin | solution.py:85
  380.3 37.3 %all_to_all.22 = f32[16,2,128]{2,1,0:T(2,128)S(1)} all-to-all(f32[16,2,128]{2,1,0:T(2,128)S(1)} %pmin.7), channel_id=1, replica_groups=mesh['bucket'=16,'ref'=32] {'bucket'}, dimensions={0} | all-to-all | bytes 32768 | tf_op jit(solution)/shard_map/all_to_all | solution.py:86
  417.6 32.6 %gather_fusion.5 = f32[3072]{0:T(1024)} fusion(f32[32,128]{1,0:T(8,128)S(1)} %bitcast.70, s32[3072]{0:T(1024)S(1)} %bitcast.71), kind=kCustom, calls=%fused_computation.5 | custom fusion | bytes 49152 | tf_op jit(solution)/shard_map/gather | solution.py:87
  (255 shorter events, 56.9 us)
Async XLA Ops:
  0.6 8.5 %copy-start.6 = (s32[3]{0:T(128)S(1)}, s32[3]{0:T(128)}, u32[]{:S(2)}) copy-start(s32[3]{0:T(128)} %constant.92) | copy-start | bytes 40
  0.6 42.7 %copy-start.5 = (s32[2]{0:T(128)S(1)}, s32[2]{0:T(128)}, u32[]{:S(2)}) copy-start(s32[2]{0:T(128)} %constant.83) | copy-start | bytes 28
  0.7 42.8 %copy-start.4 = (s32[2]{0:T(128)S(1)}, s32[2]{0:T(128)}, u32[]{:S(2)}) copy-start(s32[2]{0:T(128)} %constant.86) | copy-start | bytes 28
  0.7 42.9 %copy-start.1 = (bf16[68,3072]{1,0:T(8,128)(2,1)S(1)}, bf16[68,3072]{1,0:T(8,128)(2,1)}, u32[]{:S(2)}) copy-start(bf16[68,3072]{1,0:T(8,128)(2,1)} %param.7) | copy-start | bytes 1253380
  31.5 22.4 %all-to-all-start.1 = ((bf16[16,2,128]{2,1,0:T(2,128)(2,1)}), bf16[16,2,128]{2,1,0:T(2,128)(2,1)S(1)}, u32[]{:S(2)}, u32[]{:S(2)}) async-start(bf16[16,2,128]{2,1,0:T(2,128)(2,1)} %bitcast.51), calls=%async_computation.1 | async-start | bytes 16384 | tf_op jit(solution)/shard_map/all_to_all | solution.py:77
  52.6 8.5 %copy-start = (bf16[32,68,128]{2,0,1:T(8,128)(2,1)S(1)}, bf16[32,68,128]{2,0,1:T(8,128)(2,1)}, u32[]{:S(2)}) copy-start(bf16[32,68,128]{2,0,1:T(8,128)(2,1)} %param.9) | copy-start | bytes 1671172
  53.9 25.9 %all-to-all-start = ((bf16[32,68,128]{2,1,0:T(8,128)(2,1)}), bf16[32,68,128]{2,1,0:T(8,128)(2,1)S(1)}, u32[]{:S(2)}, u32[]{:S(2)}) async-start(bf16[32,68,128]{2,1,0:T(8,128)(2,1)} %bitcast.12), calls=%async_computation | async-start | bytes 1179648 | tf_op jit(solution)/shard_map/all_to_all | solution.py:76
  61.1 18.8 %copy-start.3 = (s32[1,1,2,768]{3,2,1,0:T(2,128)S(1)}, s32[1,1,2,768]{3,2,1,0:T(2,128)}, u32[]{:S(2)}) copy-start(s32[1,1,2,768]{3,2,1,0:T(2,128)} %param.10) | copy-start | bytes 18436
  264.2 186.0 %copy-start.2 = (f32[32,128]{1,0:T(8,128)}, f32[32,128]{1,0:T(8,128)S(1)}, u32[]{:S(2)}) copy-start(f32[32,128]{1,0:T(8,128)S(1)} %get-tuple-element.97) | copy-start | bytes 49156
where the time goes:
time: 451 us; the launch traced here: 450 us
  blocking collectives  153 us (34%)
  local copies, waits for them, and re-layouts  126 us (28%)
  matrix products  71.9 us (16%)
  other arithmetic  36.2 us (8%)
  loops' own time  24.2 us (5%)
  starting transfers between devices  19.1 us (4%)
  waiting for transfers between devices  18.2 us (4%)
    pmin x1, blocking collectives, per_device(): merged = lax.pmin(row_min, 'ref')  116 us
    dot_general x12, matrix products, advance(): jnp.einsum('pfi,pfj->pij', gen_tiles, ref_tiles, preferred_element_type=j...  71.9 us
    all_to_all x1, blocking collectives, per_device(): lax.all_to_all(merged, 'bucket', split_axis=0, concat_axis=0, tiled=True)  37.3 us
    gather x1, local copies, waits for them, and re-layouts, per_device(): gen_dist = back_rows[dest_block, slot_offset]  32.6 us
    unnamed x21, local copies, waits for them, and re-layouts  32.3 us
    another operation x1, loops' own time, tile_minima(): (row_min, col_min), ignored = lax.scan(advance, initial, offsets)  24.2 us
    gather x12, local copies, waits for them, and re-layouts, advance(): ref_tiles = ref_blocks[ref_pick]  20.7 us
    all_to_all x1, waiting for transfers between devices, per_device(): lax.all_to_all(outgoing, 'bucket', split_axis=0, concat_axis=0, tiled=True)  18.2 us
  transfers between devices with their start and end apart: 2, of which 1 were waited for; matrix products, arithmetic and copies ran while one was open for 2% of the time, Pallas kernels for 0%

commit v1 on v0

v1 whole, which is shorter than its diff:
```python
import jax
import jax.numpy as jnp
from jax import lax
from jax.experimental import pallas as pl
from jax.experimental.pallas import tpu as pltpu
from jax.sharding import PartitionSpec as P

F = 68
BLK = 128
NB = 16
NR = 32
NX = 4
NY = 8
GEN = 3072
Q = GEN // BLK
PAIRS = 768
SEND = 80
K = 128
TJ = 256
BIG = 1e30
MESH = pl.DeviceIdType.MESH
bf16 = jnp.bfloat16
f32 = jnp.float32


def iota(shape, dim):
    return lax.broadcasted_iota(jnp.int32, shape, dim)


def three(v):
    hi = v.astype(bf16).astype(f32)
    mid = (v - hi).astype(bf16).astype(f32)
    lo = (v - hi - mid).astype(bf16).astype(f32)
    return hi, mid, lo


def kernel(
    gen_ref, bid_ref, rp_ref, pairs_ref, count_ref,
    gd_ref, rd_ref,
    onehot, rank_row, blk_row, ebuf, tmp, xbuf, mrow, rft, gsend, gbuf, gop, colacc,
    rows, red, fin, back, back2,
    s1_send, s1_recv, ring_send, ring_recv, a_send, a_recv, b_send, b_recv,
):
    b = lax.axis_index("bucket")
    r = lax.axis_index("ref")
    x, y = r // NY, lax.rem(r, NY)
    to_b, half = r // 2, lax.rem(r, 2)
    same = to_b == b
    sames = same.astype(jnp.int32)

    bar = pltpu.get_barrier_semaphore()

    def greet(i, c):
        pl.semaphore_signal(bar, inc=1, device_id=(b, lax.rem(r + i, NR)), device_id_type=MESH)
        return c

    lax.fori_loop(1, NR, greet, 0)

    def greet_source(i, c):
        db, dr = i // 2, 2 * b + lax.rem(i, 2)

        @pl.when(jnp.logical_not((db == b) & (dr == r)))
        def _():
            pl.semaphore_signal(bar, inc=1, device_id=(db, dr), device_id_type=MESH)

        return c

    lax.fori_loop(0, NR, greet_source, 0)

    for q in range(Q):
        ebuf[q * NB:(q + 1) * NB, :] = (bid_ref[q:q + 1, :] == iota((NB, BLK), 0)).astype(f32).astype(bf16)
    i0, i1 = iota((BLK, 2 * BLK), 0), iota((BLK, 2 * BLK), 1)
    tri = ((i0 < i1) | (i1 >= BLK)).astype(f32).astype(bf16)
    sums = jnp.dot(ebuf[...], tri, preferred_element_type=f32)
    carry = jnp.zeros((NB, BLK), f32)
    for q in range(Q):
        e = ebuf[q * NB:(q + 1) * NB, :].astype(f32)
        part = sums[q * NB:(q + 1) * NB, :]
        rank = jnp.sum(e * (part[:, :BLK] + carry), axis=0, keepdims=True)
        carry = carry + part[:, BLK:]
        over = rank >= BLK
        off = jnp.where(over, rank - BLK, rank)
        rank_row[:, q * BLK:(q + 1) * BLK] = off
        blk = 2 * bid_ref[q:q + 1, :] + over.astype(jnp.int32)
        blk_row[:, q * BLK:(q + 1) * BLK] = blk
        onehot[:, q * BLK:(q + 1) * BLK] = (iota((BLK, BLK), 0) == off.astype(jnp.int32)).astype(f32).astype(bf16)

    mine = (blk_row[...] == r).astype(f32)
    picked = (gen_ref[...].astype(f32) * mine).astype(bf16)
    block = lax.dot_general(picked, onehot[...], (((1,), (1,)), ((), ())), preferred_element_type=f32)
    norm = jnp.sum(block * block, axis=0, keepdims=True)
    total = jnp.sum(jnp.where(iota((NB, BLK), 0) == to_b, carry, 0.0), axis=0, keepdims=True)
    slot_id = iota((1, BLK), 1) + half * BLK
    norm = jnp.where(slot_id.astype(f32) < total, norm, BIG)
    hi, mid, lo = three(norm)
    tmp[F:SEND, :] = jnp.zeros((SEND - F, BLK), f32)
    tmp[0:F, :] = block
    tmp[F:F + 1, :] = hi
    tmp[F + 1:F + 2, :] = mid
    tmp[F + 2:F + 3, :] = lo
    tmp[F + 3:F + 6, :] = jnp.ones((3, BLK), f32)
    gsend[...] = tmp[...].astype(bf16)

    pl.semaphore_wait(bar, 2 * NR - 1 - sames)

    t = 2 * b + half
    tx, ty = t // NY, lax.rem(t, NY)
    t_slot = ty * NX + tx

    def first(i):
        return pltpu.make_async_remote_copy(
            src_ref=gsend, dst_ref=gbuf.at[t_slot],
            send_sem=s1_send.at[i], recv_sem=s1_recv.at[tx],
            device_id=(to_b, i * NY + ty), device_id_type=MESH,
        )

    for i in range(NX):
        here = same & (x == i)

        @pl.when(jnp.logical_not(here))
        def _():
            first(i).start()

        @pl.when(here)
        def _():
            gbuf[t_slot] = gsend[...]

    kid = iota((K, PAIRS), 0) - SEND
    gid = jnp.where((kid >= 0) & (kid < NR), lax.rem(kid, NX) * NY + kid // NX, -1)
    live = iota((1, PAIRS), 1) < count_ref[0, 0]
    named = jnp.where(live, pairs_ref[0, 0, 0:1, :], -2)
    a_hot = (gid == named).astype(f32).astype(bf16)
    b_hot = (iota((NR, PAIRS), 0) == pairs_ref[0, 0, 1:2, :]).astype(f32).astype(bf16)
    listed = lax.dot_general(b_hot, a_hot, (((1,), (1,)), ((), ())), preferred_element_type=f32)
    lane = iota((NR, K), 1)
    mrow[...] = jnp.where(
        (lane >= SEND) & (lane < SEND + NR) & (listed < 0.5), BIG,
        jnp.where((lane >= F) & (lane < F + 3), 1.0, 0.0),
    )

    xbuf[F:K, :] = jnp.zeros((K - F, BLK), f32)

    def prepare(k, c):
        v = rp_ref[k].astype(f32)
        rh, rm, rl = three(jnp.sum(v * v, axis=0, keepdims=True))
        xbuf[0:F, :] = -2.0 * v
        xbuf[F + 3:F + 4, :] = rh
        xbuf[F + 4:F + 5, :] = rm
        xbuf[F + 5:F + 6, :] = rl
        at = pl.multiple_of(k * BLK, BLK)
        rft[pl.ds(at, BLK), :] = (xbuf[...].T + mrow[pl.ds(k, 1), :]).astype(bf16)
        return c

    lax.fori_loop(0, NR, prepare, 0)

    def settle(i, slot):
        g = lax.rem(slot, NX) * NY + slot // NX
        return pltpu.make_async_remote_copy(
            src_ref=rows.at[slot], dst_ref=red.at[r],
            send_sem=a_send, recv_sem=a_recv,
            device_id=(b, g), device_id_type=MESH,
        )

    def compute(group, is_first):
        for i in range(NX):
            slot = group * NX + i
            hot = (iota((K - SEND, BLK), 0) == slot).astype(f32).astype(bf16)
            gop[0:SEND, i * BLK:(i + 1) * BLK] = gbuf[slot]
            gop[SEND:K, i * BLK:(i + 1) * BLK] = hot

        def tile(j, acc):
            at = pl.multiple_of(j * TJ, TJ)
            d = jnp.dot(rft[pl.ds(at, TJ), :], gop[...], preferred_element_type=f32)
            acc = jnp.minimum(acc, jnp.min(d.reshape(TJ // 8, 8, NX * BLK), axis=0))
            m = jnp.minimum(
                jnp.minimum(d[:, 0:BLK], d[:, BLK:2 * BLK]),
                jnp.minimum(d[:, 2 * BLK:3 * BLK], d[:, 3 * BLK:4 * BLK]),
            )
            if not is_first:
                m = jnp.minimum(m, colacc[pl.ds(at, TJ), :])
            colacc[pl.ds(at, TJ), :] = m
            return acc

        acc = lax.fori_loop(0, NR * BLK // TJ, tile, jnp.full((8, NX * BLK), BIG, f32))
        low = jnp.min(acc, axis=0, keepdims=True)
        for i in range(NX):
            slot = group * NX + i
            rows[slot] = low[:, i * BLK:(i + 1) * BLK]
        for i in range(NX):
            slot = group * NX + i
            own = (group == y) & (x == i)

            @pl.when(jnp.logical_not(own))
            def _():
                settle(i, slot).start()

            @pl.when(own)
            def _():
                red[r] = rows[slot]

    for i in range(NX):
        src_b = (i * NY + y) // 2
        here = same & (x == i)

        @pl.when(jnp.logical_not(here))
        def _():
            first(i).wait_send()
            pltpu.make_async_remote_copy(
                src_ref=gsend, dst_ref=gbuf.at[y * NX + i],
                send_sem=s1_send.at[i], recv_sem=s1_recv.at[i],
                device_id=(src_b, r), device_id_type=MESH,
            ).wait_recv()

    def hop(way, step):
        sign = 1 if way == 0 else -1
        group = lax.rem(y - sign * (step - 1) + 2 * NY, NY)
        if step < NY // 2:
            piece = gbuf.at[pl.ds(group * NX, NX)]
        else:
            piece = gbuf.at[pl.ds(group * NX + way * (NX // 2), NX // 2)]
        to = lax.rem(y + sign + NY, NY)
        return pltpu.make_async_remote_copy(
            src_ref=piece, dst_ref=piece,
            send_sem=ring_send.at[way, step - 1], recv_sem=ring_recv.at[way, step - 1],
            device_id=(b, x * NY + to), device_id_type=MESH,
        )

    def arrival(way, step):
        sign = 1 if way == 0 else -1
        group = lax.rem(y - sign * step + 2 * NY, NY)
        if step < NY // 2:
            piece = gbuf.at[pl.ds(group * NX, NX)]
        else:
            piece = gbuf.at[pl.ds(group * NX + way * (NX // 2), NX // 2)]
        return pltpu.make_async_remote_copy(
            src_ref=piece, dst_ref=piece,
            send_sem=ring_send.at[way, step - 1], recv_sem=ring_recv.at[way, step - 1],
            device_id=(b, x * NY + lax.rem(y - sign + NY, NY)), device_id_type=MESH,
        )

    for way in range(2):
        hop(way, 1).start()
    compute(y, True)
    for step in range(1, NY // 2):
        for way in range(2):
            arrival(way, step).wait_recv()
            hop(way, step + 1).start()
        compute(lax.rem(y - step + NY, NY), False)
        compute(lax.rem(y + step, NY), False)
    for way in range(2):
        arrival(way, NY // 2).wait_recv()
    compute(lax.rem(y + NY // 2, NY), False)

    def finish(k, c):
        at = pl.multiple_of(k * BLK, BLK)
        v = colacc[pl.ds(at, BLK), :].T
        rd_ref[pl.ds(k, 1), :] = jnp.min(v, axis=0, keepdims=True) / F
        return c

    lax.fori_loop(0, NR, finish, 0)

    pltpu.make_async_copy(red.at[pl.ds(0, NR - 1)], red.at[pl.ds(0, NR - 1)], a_recv).wait()
    low = red[0]
    for i in range(1, NR):
        low = jnp.minimum(low, red[i])
    fin[0] = low / F

    def deliver(i, c):
        @pl.when(jnp.logical_not(same & (i == r)))
        def _():
            pltpu.make_async_remote_copy(
                src_ref=fin.at[0], dst_ref=back.at[t],
                send_sem=b_send, recv_sem=b_recv,
                device_id=(to_b, i), device_id_type=MESH,
            ).start()

        return c

    lax.fori_loop(0, NR, deliver, 0)

    @pl.when(same)
    def _():
        back[t] = fin[0]
        pltpu.make_async_copy(back.at[pl.ds(0, NR - 1)], back.at[pl.ds(0, NR - 1)], b_recv).wait()

    @pl.when(jnp.logical_not(same))
    def _():
        pltpu.make_async_copy(back.at[pl.ds(0, NR)], back.at[pl.ds(0, NR)], b_recv).wait()

    for i in range(NR):
        back2[i:i + 1, :] = back[i]
    hi, mid, lo = three(back2[...])
    parts = jnp.concatenate([hi, mid, lo], axis=0).astype(bf16)
    for q in range(0, Q, 4):
        cols = slice(q * BLK, (q + 4) * BLK)
        v = jnp.dot(parts, onehot[:, cols], preferred_element_type=f32)
        v = v[0:NR] + v[NR:2 * NR] + v[2 * NR:3 * NR]
        pick = iota((NR, 4 * BLK), 0) == blk_row[:, cols]
        v = jnp.sum(jnp.where(pick, v, 0.0), axis=0, keepdims=True)
        for i in range(4):
            gd_ref[q + i:q + i + 1, :] = v[:, i * BLK:(i + 1) * BLK]

    for way in range(2):
        for step in range(1, NY // 2 + 1):
            hop(way, step).wait_send()
    pltpu.make_async_copy(rows.at[pl.ds(0, NR - 1)], rows.at[pl.ds(0, NR - 1)], a_send).wait()

    @pl.when(same)
    def _():
        pltpu.make_async_copy(back.at[pl.ds(0, NR - 1)], back.at[pl.ds(0, NR - 1)], b_send).wait()

    @pl.when(jnp.logical_not(same))
    def _():
        pltpu.make_async_copy(back.at[pl.ds(0, NR)], back.at[pl.ds(0, NR)], b_send).wait()


def per_device(gen_points, bucket_id, ref_points, block_pairs, pair_count):
    vmem = pl.BlockSpec(memory_space=pltpu.VMEM)
    dma = pltpu.SemaphoreType.DMA
    gd, rd = pl.pallas_call(
        kernel,
        out_shape=(
            jax.ShapeDtypeStruct((Q, BLK), f32),
            jax.ShapeDtypeStruct((NR, BLK), f32),
        ),
        in_specs=[vmem] * 4 + [pl.BlockSpec(memory_space=pltpu.SMEM)],
        out_specs=(vmem, vmem),
        scratch_shapes=[
            pltpu.VMEM((BLK, GEN), bf16),
            pltpu.VMEM((1, GEN), f32),
            pltpu.VMEM((1, GEN), jnp.int32),
            pltpu.VMEM((Q * NB, BLK), bf16),
            pltpu.VMEM((SEND, BLK), f32),
            pltpu.VMEM((K, BLK), f32),
            pltpu.VMEM((NR, K), f32),
            pltpu.VMEM((NR * BLK, K), bf16),
            pltpu.VMEM((SEND, BLK), bf16),
            pltpu.VMEM((NR, SEND, BLK), bf16),
            pltpu.VMEM((K, NX * BLK), bf16),
            pltpu.VMEM((NR * BLK, BLK), f32),
            pltpu.VMEM((NR, 1, BLK), f32),
            pltpu.VMEM((NR, 1, BLK), f32),
            pltpu.VMEM((1, 1, BLK), f32),
            pltpu.VMEM((NR, 1, BLK), f32),
            pltpu.VMEM((NR, BLK), f32),
            dma((NX,)), dma((NX,)), dma((2, NY // 2)), dma((2, NY // 2)),
            dma, dma, dma, dma,
        ],
        compiler_params=pltpu.CompilerParams(
            collective_id=0, has_side_effects=True, vmem_limit_bytes=48 * 2**20
        ),
        cost_estimate=pl.CostEstimate(
            flops=2 * 4096 * 4096 * 128, bytes_accessed=2**21, transcendentals=0
        ),
        name="chamfer",
    )(gen_points, bucket_id.reshape(Q, BLK), ref_points, block_pairs, pair_count)
    return gd.reshape(GEN), rd


def solution(mesh):
    return jax.shard_map(
        per_device,
        mesh=mesh,
        in_specs=(
            P(None, "bucket"),
            P("bucket"),
            P(("bucket", "ref"), None, None),
            P("bucket", "ref", None, None),
            P("bucket", "ref"),
        ),
        out_specs=(P("bucket"), P(("bucket", "ref"), None)),
        check_vma=False,
    )
```

time: 451 us -> 71.3 us (0.16)
  blocking collectives: 153 us -> 0 us
  local copies, waits for them, and re-layouts: 126 us -> 2.54 us
  matrix products: 71.9 us -> 0 us
  Pallas kernels: 0 us -> 67.2 us
  other arithmetic: 36.2 us -> 0 us
  loops' own time: 24.2 us -> 0 us
  starting transfers between devices: 19.1 us -> 0 us
  waiting for transfers between devices: 18.2 us -> 0 us
    pmin x1 -> x0, blocking collectives: 116 us -> none  [per_device(): merged = lax.pmin(row_min, 'ref')]
    gather x61 -> x0, local copies, waits for them, and re-layouts: 84.2 us -> none  [the longest x1 32.6 us: per_device(): gen_dist = back_rows[dest_block, slot_offset]]
    dot_general x12 -> x0, matrix products: 71.9 us -> none  [advance(): jnp.einsum('pfi,pfj->pij', gen_tiles, ref_tiles, preferred_element_type=j...]
    pallas_call x0 -> x1, Pallas kernels: none -> 67.2 us  [per_device(): pl.pallas_call(kernel, out_shape=(jax.ShapeDtypeStruct((Q, BLK), f32), ja...]
    all_to_all x1 -> x0, blocking collectives: 37.3 us -> none  [per_device(): lax.all_to_all(merged, 'bucket', split_axis=0, concat_axis=0, tiled=True)]
    unnamed x21 -> x9, local copies, waits for them, and re-layouts: 32.3 us -> 2.54 us
    another operation x1 -> x0, loops' own time: 24.2 us -> none  [tile_minima(): (row_min, col_min), ignored = lax.scan(advance, initial, offsets)]
    all_to_all x2 -> x0, starting transfers between devices: 19.1 us -> none  [the longest x1 11.8 us: per_device(): lax.all_to_all(live_flags, 'bucket', split_axis=0, concat_axis=0, tiled=T...]
  transfers between devices with their start and end apart: 2 -> 0, of which waited for: 1 -> 0; matrix products, arithmetic and copies ran while one was open for 2% -> 0% of each run, Pallas kernels for 0% -> 0%
where the time goes in v1:
time: 71.3 us; the launch traced here: 71.1 us
  Pallas kernels  67.2 us (94%)
  local copies, waits for them, and re-layouts  2.54 us (4%)
  between operations  1.34 us (2%)
    pallas_call x1, Pallas kernels, per_device(): pl.pallas_call(kernel, out_shape=(jax.ShapeDtypeStruct((Q, BLK), f32), ja...  67.2 us
    unnamed x9, local copies, waits for them, and re-layouts  2.54 us

profile of v1, /device:TPU:1, one launch (start us, length us, event | category | flops | bytes accessed | tf_op | source)
XLA Modules:
  0.0 71.1 jit_solution(2330588234119107768)
XLA Ops:
  1.3 0.0 copy-start
  1.3 0.0 copy-start.1
  1.3 0.0 copy-start.2
  1.3 1.3 %copy.7.rp_ref = bf16[32,68,128]{2,1,0:T(8,128)(2,1)S(1)} copy(bf16[32,68,128]{2,0,1:T(8,128)(2,1)} %param.7) | data formatting | bytes 1114112 | tf_op args[2]
  2.6 0.0 copy-done
  2.6 0.0 copy-done.1
  2.7 0.0 copy-done.2
  2.7 67.2 %chamfer.1 = (f32[24,128]{1,0:T(8,128)S(1)}, f32[32,128]{1,0:T(8,128)S(1)}) custom-call(bf16[68,3072]{1,0:T(8,128)(2,1)S(1)} %copy-done, s32[24,128]{1,0:T(8,128)S(1)} %bitcast.3, bf16[32,68,128]{2,1,0:T(8,128)(2,1)S(1)} %copy.7.rp_ref, s32[1,1,2,768]{3,2,1,0:T(2,128)S(1)} %copy-done.2, s32[1,1]{1,0:T(1,128)S(6)} %copy.10.count_ref), custom_call_target="tpu_custom_call" | custom-call | flops 4294967296 | bytes 2097152 | tf_op jit(solution)/shard_map/chamfer/pallas_call | solution.py:320
  69.9 0.6 copy.11
  70.5 0.6 copy.12
Async XLA Ops:
  1.3 1.4 %copy-start = (bf16[68,3072]{1,0:T(8,128)(2,1)S(1)}, bf16[68,3072]{1,0:T(8,128)(2,1)}, u32[]{:S(2)}) copy-start(bf16[68,3072]{1,0:T(8,128)(2,1)} %gen_ref.1) | copy-start | bytes 1253380
  1.3 1.4 %copy-start.1 = (s32[3072]{0:T(1024)S(1)}, s32[3072]{0:T(1024)}, u32[]{:S(2)}) copy-start(s32[3072]{0:T(1024)} %param.6) | copy-start | bytes 36868
  1.3 1.4 %copy-start.2 = (s32[1,1,2,768]{3,2,1,0:T(2,128)S(1)}, s32[1,1,2,768]{3,2,1,0:T(2,128)}, u32[]{:S(2)}) copy-start(s32[1,1,2,768]{3,2,1,0:T(2,128)} %pairs_ref.1) | copy-start | bytes 18436

commit v2 on v1

--- a/solution.py
+++ b/solution.py
@@ -16,7 +16,7 @@
 PAIRS = 768
 SEND = 80
 K = 128
-TJ = 256
+UN = 8
 BIG = 1e30
 MESH = pl.DeviceIdType.MESH
 bf16 = jnp.bfloat16
@@ -37,6 +37,7 @@
 def kernel(
     gen_ref, bid_ref, rp_ref, pairs_ref, count_ref,
     gd_ref, rd_ref,
+    rpf, rnorm,
     onehot, rank_row, blk_row, ebuf, tmp, xbuf, mrow, rft, gsend, gbuf, gop, colacc,
     rows, red, fin, back, back2,
     s1_send, s1_recv, ring_send, ring_recv, a_send, a_recv, b_send, b_recv,
@@ -138,20 +139,27 @@
         jnp.where((lane >= F) & (lane < F + 3), 1.0, 0.0),
     )
 
-    xbuf[F:K, :] = jnp.zeros((K - F, BLK), f32)
-
-    def prepare(k, c):
-        v = rp_ref[k].astype(f32)
-        rh, rm, rl = three(jnp.sum(v * v, axis=0, keepdims=True))
-        xbuf[0:F, :] = -2.0 * v
-        xbuf[F + 3:F + 4, :] = rh
-        xbuf[F + 4:F + 5, :] = rm
-        xbuf[F + 5:F + 6, :] = rl
-        at = pl.multiple_of(k * BLK, BLK)
-        rft[pl.ds(at, BLK), :] = (xbuf[...].T + mrow[pl.ds(k, 1), :]).astype(bf16)
-        return c
-
-    lax.fori_loop(0, NR, prepare, 0)
+    v = rp_ref[...].astype(f32)
+    for i, part in enumerate(three(jnp.sum(v * v, axis=0))):
+        rnorm[i] = part
+    rpf[...] = (-2.0 * v).reshape(F * NR, BLK)
+    for u in range(UN):
+        xbuf[u, F:K, :] = jnp.zeros((K - F, BLK), f32)
+
+    def prepare(first_k, c):
+        for u in range(UN):
+            k = first_k * UN + u
+            xbuf[u, 0:F, :] = rpf[pl.ds(k, F, stride=NR), :]
+            for i in range(3):
+                xbuf[u, F + 3 + i:F + 4 + i, :] = rnorm[i, pl.ds(k, 1), :]
+        for u in range(UN):
+            k = first_k * UN + u
+            at = pl.multiple_of(k * BLK, BLK)
+            rft[pl.ds(at, BLK), :] = xbuf[u].astype(bf16).T + mrow[pl.ds(k, 1), :].astype(bf16)
+            colacc[pl.ds(at, BLK), :] = jnp.full((BLK, BLK), 4 * BIG, f32)
+        return c
+
+    lax.fori_loop(0, NR // UN // 2, prepare, 0)
 
     def settle(i, slot):
         g = lax.rem(slot, NX) * NY + slot // NX
@@ -161,27 +169,19 @@
             device_id=(b, g), device_id_type=MESH,
         )
 
-    def compute(group, is_first):
+    def compute(group):
         for i in range(NX):
             slot = group * NX + i
             hot = (iota((K - SEND, BLK), 0) == slot).astype(f32).astype(bf16)
             gop[0:SEND, i * BLK:(i + 1) * BLK] = gbuf[slot]
             gop[SEND:K, i * BLK:(i + 1) * BLK] = hot
-
-        def tile(j, acc):
-            at = pl.multiple_of(j * TJ, TJ)
-            d = jnp.dot(rft[pl.ds(at, TJ), :], gop[...], preferred_element_type=f32)
-            acc = jnp.minimum(acc, jnp.min(d.reshape(TJ // 8, 8, NX * BLK), axis=0))
-            m = jnp.minimum(
-                jnp.minimum(d[:, 0:BLK], d[:, BLK:2 * BLK]),
-                jnp.minimum(d[:, 2 * BLK:3 * BLK], d[:, 3 * BLK:4 * BLK]),
-            )
-            if not is_first:
-                m = jnp.minimum(m, colacc[pl.ds(at, TJ), :])
-            colacc[pl.ds(at, TJ), :] = m
-            return acc
-
-        acc = lax.fori_loop(0, NR * BLK // TJ, tile, jnp.full((8, NX * BLK), BIG, f32))
+        d = jnp.dot(rft[...], gop[...], preferred_element_type=f32)
+        acc = jnp.min(d.reshape(NR * BLK // 8, 8, NX * BLK), axis=0)
+        m = jnp.minimum(
+            jnp.minimum(d[:, 0:BLK], d[:, BLK:2 * BLK]),
+            jnp.minimum(d[:, 2 * BLK:3 * BLK], d[:, 3 * BLK:4 * BLK]),
+        )
+        colacc[...] = jnp.minimum(colacc[...], m)
         low = jnp.min(acc, axis=0, keepdims=True)
         for i in range(NX):
             slot = group * NX + i
@@ -211,13 +211,13 @@
                 device_id=(src_b, r), device_id_type=MESH,
             ).wait_recv()
 
-    def hop(way, step):
-        sign = 1 if way == 0 else -1
-        group = lax.rem(y - sign * (step - 1) + 2 * NY, NY)
-        if step < NY // 2:
+    def ring(way, step, behind, last):
+        sign = 1 - 2 * way
+        group = lax.rem(y - sign * (step - behind) + 2 * NY, NY)
+        if last:
+            piece = gbuf.at[pl.ds(group * NX + way * (NX // 2), NX // 2)]
+        else:
             piece = gbuf.at[pl.ds(group * NX, NX)]
-        else:
-            piece = gbuf.at[pl.ds(group * NX + way * (NX // 2), NX // 2)]
         to = lax.rem(y + sign + NY, NY)
         return pltpu.make_async_remote_copy(
             src_ref=piece, dst_ref=piece,
@@ -225,39 +225,46 @@
             device_id=(b, x * NY + to), device_id_type=MESH,
         )
 
-    def arrival(way, step):
-        sign = 1 if way == 0 else -1
-        group = lax.rem(y - sign * step + 2 * NY, NY)
-        if step < NY // 2:
-            piece = gbuf.at[pl.ds(group * NX, NX)]
-        else:
-            piece = gbuf.at[pl.ds(group * NX + way * (NX // 2), NX // 2)]
-        return pltpu.make_async_remote_copy(
-            src_ref=piece, dst_ref=piece,
-            send_sem=ring_send.at[way, step - 1], recv_sem=ring_recv.at[way, step - 1],
-            device_id=(b, x * NY + lax.rem(y - sign + NY, NY)), device_id_type=MESH,
-        )
-
     for way in range(2):
-        hop(way, 1).start()
-    compute(y, True)
-    for step in range(1, NY // 2):
-        for way in range(2):
-            arrival(way, step).wait_recv()
-            hop(way, step + 1).start()
-        compute(lax.rem(y - step + NY, NY), False)
-        compute(lax.rem(y + step, NY), False)
-    for way in range(2):
-        arrival(way, NY // 2).wait_recv()
-    compute(lax.rem(y + NY // 2, NY), False)
-
-    def finish(k, c):
-        at = pl.multiple_of(k * BLK, BLK)
-        v = colacc[pl.ds(at, BLK), :].T
-        rd_ref[pl.ds(k, 1), :] = jnp.min(v, axis=0, keepdims=True) / F
-        return c
-
-    lax.fori_loop(0, NR, finish, 0)
+        ring(way, 1, 1, False).start()
+    lax.fori_loop(NR // UN // 2, NR // UN, prepare, 0)
+
+    def group_step(i, c):
+        step = (i + 1) // 2
+        odd = lax.rem(i, 2)
+
+        @pl.when((odd == 1) & (step < NY // 2))
+        def _():
+            for way in range(2):
+                ring(way, step, 0, False).wait_recv()
+
+                @pl.when(step + 1 < NY // 2)
+                def _():
+                    ring(way, step + 1, 1, False).start()
+
+                @pl.when(step + 1 == NY // 2)
+                def _():
+                    ring(way, step + 1, 1, True).start()
+
+        @pl.when(step == NY // 2)
+        def _():
+            for way in range(2):
+                ring(way, step, 0, True).wait_recv()
+
+        compute(lax.rem(y + (1 - 2 * odd) * step + NY, NY))
+        return c
+
+    lax.fori_loop(0, NY, group_step, 0)
+
+    def finish(first_k, c):
+        for u in range(UN):
+            k = first_k * UN + u
+            at = pl.multiple_of(k * BLK, BLK)
+            v = colacc[pl.ds(at, BLK), :].T
+            rd_ref[pl.ds(k, 1), :] = jnp.min(v, axis=0, keepdims=True) / F
+        return c
+
+    lax.fori_loop(0, NR // UN // 2, finish, 0)
 
     pltpu.make_async_copy(red.at[pl.ds(0, NR - 1)], red.at[pl.ds(0, NR - 1)], a_recv).wait()
     low = red[0]
@@ -277,6 +284,7 @@
         return c
 
     lax.fori_loop(0, NR, deliver, 0)
+    lax.fori_loop(NR // UN // 2, NR // UN, finish, 0)
 
     @pl.when(same)
     def _():
@@ -302,7 +310,7 @@
 
     for way in range(2):
         for step in range(1, NY // 2 + 1):
-            hop(way, step).wait_send()
+            ring(way, step, 1, step == NY // 2).wait_send()
     pltpu.make_async_copy(rows.at[pl.ds(0, NR - 1)], rows.at[pl.ds(0, NR - 1)], a_send).wait()
 
     @pl.when(same)
@@ -326,12 +334,14 @@
         in_specs=[vmem] * 4 + [pl.BlockSpec(memory_space=pltpu.SMEM)],
         out_specs=(vmem, vmem),
         scratch_shapes=[
+            pltpu.VMEM((F * NR, BLK), f32),
+            pltpu.VMEM((3, NR, BLK), f32),
             pltpu.VMEM((BLK, GEN), bf16),
             pltpu.VMEM((1, GEN), f32),
             pltpu.VMEM((1, GEN), jnp.int32),
             pltpu.VMEM((Q * NB, BLK), bf16),
             pltpu.VMEM((SEND, BLK), f32),
-            pltpu.VMEM((K, BLK), f32),
+            pltpu.VMEM((UN, K, BLK), f32),
             pltpu.VMEM((NR, K), f32),
             pltpu.VMEM((NR * BLK, K), bf16),
             pltpu.VMEM((SEND, BLK), bf16),
@@ -353,7 +363,10 @@
             flops=2 * 4096 * 4096 * 128, bytes_accessed=2**21, transcendentals=0
         ),
         name="chamfer",
-    )(gen_points, bucket_id.reshape(Q, BLK), ref_points, block_pairs, pair_count)
+    )(
+        gen_points, bucket_id.reshape(Q, BLK), ref_points.transpose(1, 0, 2), block_pairs,
+        pair_count,
+    )
     return gd.reshape(GEN), rd
 
 

time: 71.3 us -> 62.4 us (0.88)
  Pallas kernels: 67.2 us -> 56.1 us
  local copies, waits for them, and re-layouts: 2.54 us -> 4.66 us
    pallas_call x1, Pallas kernels: 67.2 us -> 56.1 us  [per_device(): pl.pallas_call(kernel, out_shape=(jax.ShapeDtypeStruct((Q, BLK), f32), ja...]
    unnamed x9 -> x10, local copies, waits for them, and re-layouts: 2.54 us -> 4.66 us
where the time goes in v2:
time: 62.4 us; the launch traced here: 62.1 us
  Pallas kernels  56.1 us (90%)
  local copies, waits for them, and re-layouts  4.66 us (7%)
  between operations  1.3 us (2%)
    pallas_call x1, Pallas kernels, per_device(): pl.pallas_call(kernel, out_shape=(jax.ShapeDtypeStruct((Q, BLK), f32), ja...  56.1 us
    unnamed x10, local copies, waits for them, and re-layouts  4.66 us

profile of v2, /device:TPU:1, one launch (start us, length us, event | category | flops | bytes accessed | tf_op | source)
XLA Modules:
  0.0 62.1 jit_solution(16619915656591293015)
XLA Ops:
  1.3 0.0 copy-start
  1.3 1.0 %copy-done = bf16[32,68,128]{2,0,1:T(8,128)(2,1)S(1)} copy-done((bf16[32,68,128]{2,0,1:T(8,128)(2,1)S(1)}, bf16[32,68,128]{2,0,1:T(8,128)(2,1)}, u32[]{:S(2)}) %copy-start) | copy-done | bytes 557080
  2.3 0.0 copy-start.1
  2.3 1.0 %copy-done.1 = bf16[68,3072]{1,0:T(8,128)(2,1)S(1)} copy-done((bf16[68,3072]{1,0:T(8,128)(2,1)S(1)}, bf16[68,3072]{1,0:T(8,128)(2,1)}, u32[]{:S(2)}) %copy-start.1) | copy-done | bytes 417816
  3.3 0.0 copy-start.2
  3.3 0.7 %copy-done.2 = s32[3072]{0:T(1024)S(1)} copy-done((s32[3072]{0:T(1024)S(1)}, s32[3072]{0:T(1024)}, u32[]{:S(2)}) %copy-start.2) | copy-done | bytes 12312
  4.1 0.0 copy-start.3
  4.1 0.7 %copy-done.3 = s32[1,1,2,768]{3,2,1,0:T(2,128)S(1)} copy-done((s32[1,1,2,768]{3,2,1,0:T(2,128)S(1)}, s32[1,1,2,768]{3,2,1,0:T(2,128)}, u32[]{:S(2)}) %copy-start.3) | copy-done | bytes 6168
  4.7 56.1 %chamfer.1 = (f32[24,128]{1,0:T(8,128)S(1)}, f32[32,128]{1,0:T(8,128)S(1)}) custom-call(bf16[68,3072]{1,0:T(8,128)(2,1)S(1)} %copy-done.1, s32[24,128]{1,0:T(8,128)S(1)} %bitcast.5, bf16[68,32,128]{2,1,0:T(8,128)(2,1)S(1)} %bitcast.4, s32[1,1,2,768]{3,2,1,0:T(2,128)S(1)} %copy-done.3, s32[1,1]{1,0:T(1,128)S(6)} %copy.9.count_ref), custom_call_target="tpu_custom_call" | custom-call | flops 4294967296 | bytes 2097152 | tf_op jit(solution)/shard_map/chamfer/pallas_call | solution.py:328
  60.8 0.6 copy.10
  61.4 0.6 copy.11
Async XLA Ops:
  1.3 1.1 %copy-start = (bf16[32,68,128]{2,0,1:T(8,128)(2,1)S(1)}, bf16[32,68,128]{2,0,1:T(8,128)(2,1)}, u32[]{:S(2)}) copy-start(bf16[32,68,128]{2,0,1:T(8,128)(2,1)} %param.7) | copy-start | bytes 1671172
  2.3 1.0 %copy-start.1 = (bf16[68,3072]{1,0:T(8,128)(2,1)S(1)}, bf16[68,3072]{1,0:T(8,128)(2,1)}, u32[]{:S(2)}) copy-start(bf16[68,3072]{1,0:T(8,128)(2,1)} %gen_ref.1) | copy-start | bytes 1253380
  3.3 0.7 %copy-start.2 = (s32[3072]{0:T(1024)S(1)}, s32[3072]{0:T(1024)}, u32[]{:S(2)}) copy-start(s32[3072]{0:T(1024)} %param.6) | copy-start | bytes 36868
  4.1 0.7 %copy-start.3 = (s32[1,1,2,768]{3,2,1,0:T(2,128)S(1)}, s32[1,1,2,768]{3,2,1,0:T(2,128)}, u32[]{:S(2)}) copy-start(s32[1,1,2,768]{3,2,1,0:T(2,128)} %pairs_ref.1) | copy-start | bytes 18436

commit v3 on v2

--- a/solution.py
+++ b/solution.py
@@ -35,39 +35,48 @@
 
 
 def kernel(
-    gen_ref, bid_ref, rp_ref, pairs_ref, count_ref,
+    gen_hbm, bid_hbm, rp_hbm, pairs_hbm, count_ref,
     gd_ref, rd_ref,
+    gen_ref, bid_ref, rp_ref, pairs_ref, in_sem, picked,
     rpf, rnorm,
     onehot, rank_row, blk_row, ebuf, tmp, xbuf, mrow, rft, gsend, gbuf, gop, colacc,
-    rows, red, fin, back, back2,
-    s1_send, s1_recv, ring_send, ring_recv, a_send, a_recv, b_send, b_recv,
+    rows, red_y, low_y, red_x, fin, back, back2,
+    s1_send, s1_recv, ring_send, ring_recv, y_send, y_recv, x_send, x_recv, z_send, z_recv,
 ):
     b = lax.axis_index("bucket")
     r = lax.axis_index("ref")
     x, y = r // NY, lax.rem(r, NY)
-    to_b, half = r // 2, lax.rem(r, 2)
-    same = to_b == b
-    sames = same.astype(jnp.int32)
+    half, turn = lax.rem(y, 2), y // 2
+    mates = [4 * i + lax.rem(turn - b + NB, 4) for i in range(NX)]
+
+    loads = [
+        pltpu.make_async_copy(src, dst, in_sem.at[i])
+        for i, (src, dst) in enumerate(
+            [(bid_hbm, bid_ref), (gen_hbm, gen_ref), (pairs_hbm, pairs_ref), (rp_hbm, rp_ref)]
+        )
+    ]
+    for copy in loads:
+        copy.start()
 
     bar = pltpu.get_barrier_semaphore()
 
-    def greet(i, c):
-        pl.semaphore_signal(bar, inc=1, device_id=(b, lax.rem(r + i, NR)), device_id_type=MESH)
-        return c
-
-    lax.fori_loop(1, NR, greet, 0)
-
-    def greet_source(i, c):
-        db, dr = i // 2, 2 * b + lax.rem(i, 2)
-
-        @pl.when(jnp.logical_not((db == b) & (dr == r)))
-        def _():
-            pl.semaphore_signal(bar, inc=1, device_id=(db, dr), device_id_type=MESH)
-
-        return c
-
-    lax.fori_loop(0, NR, greet_source, 0)
-
+    def at_x(i):
+        return (b, lax.rem(x + i, NX) * NY + y)
+
+    def at_y(i):
+        return (b, x * NY + lax.rem(y + i, NY))
+
+    def at_z(i):
+        return (lax.rem(b + i, NB), r)
+
+    for peer, count in ((at_z, NB), (at_y, NY), (at_x, NX)):
+        def greet(i, c, peer=peer):
+            pl.semaphore_signal(bar, inc=1, device_id=peer(i), device_id_type=MESH)
+            return c
+
+        lax.fori_loop(1, count, greet, 0)
+
+    loads[0].wait()
     for q in range(Q):
         ebuf[q * NB:(q + 1) * NB, :] = (bid_ref[q:q + 1, :] == iota((NB, BLK), 0)).astype(f32).astype(bf16)
     i0, i1 = iota((BLK, 2 * BLK), 0), iota((BLK, 2 * BLK), 1)
@@ -86,48 +95,52 @@
         blk_row[:, q * BLK:(q + 1) * BLK] = blk
         onehot[:, q * BLK:(q + 1) * BLK] = (iota((BLK, BLK), 0) == off.astype(jnp.int32)).astype(f32).astype(bf16)
 
-    mine = (blk_row[...] == r).astype(f32)
-    picked = (gen_ref[...].astype(f32) * mine).astype(bf16)
-    block = lax.dot_general(picked, onehot[...], (((1,), (1,)), ((), ())), preferred_element_type=f32)
-    norm = jnp.sum(block * block, axis=0, keepdims=True)
-    total = jnp.sum(jnp.where(iota((NB, BLK), 0) == to_b, carry, 0.0), axis=0, keepdims=True)
-    slot_id = iota((1, BLK), 1) + half * BLK
-    norm = jnp.where(slot_id.astype(f32) < total, norm, BIG)
-    hi, mid, lo = three(norm)
-    tmp[F:SEND, :] = jnp.zeros((SEND - F, BLK), f32)
-    tmp[0:F, :] = block
-    tmp[F:F + 1, :] = hi
-    tmp[F + 1:F + 2, :] = mid
-    tmp[F + 2:F + 3, :] = lo
-    tmp[F + 3:F + 6, :] = jnp.ones((3, BLK), f32)
-    gsend[...] = tmp[...].astype(bf16)
-
-    pl.semaphore_wait(bar, 2 * NR - 1 - sames)
-
-    t = 2 * b + half
-    tx, ty = t // NY, lax.rem(t, NY)
-    t_slot = ty * NX + tx
+    loads[1].wait()
+    for i in range(NX):
+        mine = (blk_row[...] == 2 * mates[i] + half).astype(f32).astype(bf16)
+        picked[i, 0:F, :] = gen_ref[...] * mine
+        picked[i, F:SEND, :] = jnp.zeros((SEND - F, GEN), bf16)
+    blocks = lax.dot_general(
+        picked[...].reshape(NX * SEND, GEN), onehot[...], (((1,), (1,)), ((), ())),
+        preferred_element_type=f32,
+    )
+    for i in range(NX):
+        block = blocks[i * SEND:(i + 1) * SEND]
+        norm = jnp.sum(block * block, axis=0, keepdims=True)
+        total = jnp.sum(jnp.where(iota((NB, BLK), 0) == mates[i], carry, 0.0), axis=0, keepdims=True)
+        slot_id = iota((1, BLK), 1) + half * BLK
+        norm = jnp.where(slot_id.astype(f32) < total, norm, BIG)
+        tmp[i] = block
+        for j, part in enumerate(three(norm)):
+            tmp[i, F + j:F + j + 1, :] = part
+        tmp[i, F + 3:F + 6, :] = jnp.ones((3, BLK), f32)
+        gsend[i] = tmp[i].astype(bf16)
+
+    pl.semaphore_wait(bar, NB + NX + NY - 3)
+
+    my_slot = y * NX + b // 4
 
     def first(i):
         return pltpu.make_async_remote_copy(
-            src_ref=gsend, dst_ref=gbuf.at[t_slot],
-            send_sem=s1_send.at[i], recv_sem=s1_recv.at[tx],
-            device_id=(to_b, i * NY + ty), device_id_type=MESH,
+            src_ref=gsend.at[i], dst_ref=gbuf.at[my_slot],
+            send_sem=s1_send.at[i], recv_sem=s1_recv.at[b // 4],
+            device_id=(mates[i], r), device_id_type=MESH,
         )
 
     for i in range(NX):
-        here = same & (x == i)
-
-        @pl.when(jnp.logical_not(here))
+
+        @pl.when(mates[i] != b)
         def _():
             first(i).start()
 
-        @pl.when(here)
-        def _():
-            gbuf[t_slot] = gsend[...]
-
+        @pl.when(mates[i] == b)
+        def _():
+            gbuf[my_slot] = gsend[i]
+
+    loads[2].wait()
     kid = iota((K, PAIRS), 0) - SEND
-    gid = jnp.where((kid >= 0) & (kid < NR), lax.rem(kid, NX) * NY + kid // NX, -1)
+    gid = 8 * (kid & 3) + 2 * (((kid >> 3) - b + NB) & 3) + ((kid >> 2) & 1)
+    gid = jnp.where((kid >= 0) & (kid < NR), gid, -1)
     live = iota((1, PAIRS), 1) < count_ref[0, 0]
     named = jnp.where(live, pairs_ref[0, 0, 0:1, :], -2)
     a_hot = (gid == named).astype(f32).astype(bf16)
@@ -139,6 +152,7 @@
         jnp.where((lane >= F) & (lane < F + 3), 1.0, 0.0),
     )
 
+    loads[3].wait()
     v = rp_ref[...].astype(f32)
     for i, part in enumerate(three(jnp.sum(v * v, axis=0))):
         rnorm[i] = part
@@ -161,15 +175,15 @@
 
     lax.fori_loop(0, NR // UN // 2, prepare, 0)
 
-    def settle(i, slot):
-        g = lax.rem(slot, NX) * NY + slot // NX
-        return pltpu.make_async_remote_copy(
-            src_ref=rows.at[slot], dst_ref=red.at[r],
-            send_sem=a_send, recv_sem=a_recv,
-            device_id=(b, g), device_id_type=MESH,
-        )
-
-    def compute(group):
+    def along_y(start, size):
+        for k in range(1, NY):
+            pltpu.make_async_remote_copy(
+                src_ref=rows.at[pl.ds(start, size)], dst_ref=red_y.at[y, pl.ds(start, size)],
+                send_sem=y_send, recv_sem=y_recv,
+                device_id=at_y(k), device_id_type=MESH,
+            ).start()
+
+    def compute(i_step, group):
         for i in range(NX):
             slot = group * NX + i
             hot = (iota((K - SEND, BLK), 0) == slot).astype(f32).astype(bf16)
@@ -184,31 +198,17 @@
         colacc[...] = jnp.minimum(colacc[...], m)
         low = jnp.min(acc, axis=0, keepdims=True)
         for i in range(NX):
-            slot = group * NX + i
-            rows[slot] = low[:, i * BLK:(i + 1) * BLK]
-        for i in range(NX):
-            slot = group * NX + i
-            own = (group == y) & (x == i)
-
-            @pl.when(jnp.logical_not(own))
-            def _():
-                settle(i, slot).start()
-
-            @pl.when(own)
-            def _():
-                red[r] = rows[slot]
+            rows[i_step * NX + i] = low[:, i * BLK:(i + 1) * BLK]
 
     for i in range(NX):
-        src_b = (i * NY + y) // 2
-        here = same & (x == i)
-
-        @pl.when(jnp.logical_not(here))
+
+        @pl.when(mates[i] != b)
         def _():
             first(i).wait_send()
             pltpu.make_async_remote_copy(
-                src_ref=gsend, dst_ref=gbuf.at[y * NX + i],
+                src_ref=gsend.at[i], dst_ref=gbuf.at[y * NX + i],
                 send_sem=s1_send.at[i], recv_sem=s1_recv.at[i],
-                device_id=(src_b, r), device_id_type=MESH,
+                device_id=(mates[i], r), device_id_type=MESH,
             ).wait_recv()
 
     def ring(way, step, behind, last):
@@ -251,7 +251,16 @@
             for way in range(2):
                 ring(way, step, 0, True).wait_recv()
 
-        compute(lax.rem(y + (1 - 2 * odd) * step + NY, NY))
+        compute(i, lax.rem(y + (1 - 2 * odd) * step + NY, NY))
+
+        @pl.when(i == 5)
+        def _():
+            along_y(0, 6 * NX)
+
+        @pl.when(i == 7)
+        def _():
+            along_y(6 * NX, 2 * NX)
+
         return c
 
     lax.fori_loop(0, NY, group_step, 0)
@@ -266,34 +275,42 @@
 
     lax.fori_loop(0, NR // UN // 2, finish, 0)
 
-    pltpu.make_async_copy(red.at[pl.ds(0, NR - 1)], red.at[pl.ds(0, NR - 1)], a_recv).wait()
-    low = red[0]
-    for i in range(1, NR):
-        low = jnp.minimum(low, red[i])
-    fin[0] = low / F
+    pltpu.make_async_copy(red_y.at[pl.ds(0, NY - 1)], red_y.at[pl.ds(0, NY - 1)], y_recv).wait()
+    order = {0: 0, 7: 1, 1: 2, 6: 3, 2: 4, 5: 5, 3: 6, 4: 7}
+    for ahead in range(NY):
+        at = order[ahead] * NX
+        low = rows[at:at + NX]
+        for k in range(1, NY):
+            at = order[(ahead - k) % NY] * NX
+            low = jnp.minimum(low, red_y[lax.rem(y + k, NY), at:at + NX])
+        low_y[pl.ds(lax.rem(y + ahead, NY) * NX, NX)] = low
+
+    for k in range(1, NX):
+        pltpu.make_async_remote_copy(
+            src_ref=low_y, dst_ref=red_x.at[x],
+            send_sem=x_send, recv_sem=x_recv, device_id=at_x(k), device_id_type=MESH,
+        ).start()
+    lax.fori_loop(NR // UN // 2, NR // UN, finish, 0)
+    pltpu.make_async_copy(red_x.at[pl.ds(0, NX - 1)], red_x.at[pl.ds(0, NX - 1)], x_recv).wait()
+    for s in range(NB):
+        for h in range(2):
+            slot = (2 * lax.rem(b + s, 4) + h) * NX + s // 4
+            low = low_y[slot]
+            for k in range(1, NX):
+                low = jnp.minimum(low, red_x[lax.rem(x + k, NX), slot])
+            fin[2 * s + h] = low / F
 
     def deliver(i, c):
-        @pl.when(jnp.logical_not(same & (i == r)))
-        def _():
-            pltpu.make_async_remote_copy(
-                src_ref=fin.at[0], dst_ref=back.at[t],
-                send_sem=b_send, recv_sem=b_recv,
-                device_id=(to_b, i), device_id_type=MESH,
-            ).start()
-
+        s = lax.rem(b + i, NB)
+        pltpu.make_async_remote_copy(
+            src_ref=fin.at[pl.ds(2 * s, 2)], dst_ref=back.at[pl.ds(2 * b, 2)],
+            send_sem=z_send, recv_sem=z_recv, device_id=(s, r), device_id_type=MESH,
+        ).start()
         return c
 
-    lax.fori_loop(0, NR, deliver, 0)
-    lax.fori_loop(NR // UN // 2, NR // UN, finish, 0)
-
-    @pl.when(same)
-    def _():
-        back[t] = fin[0]
-        pltpu.make_async_copy(back.at[pl.ds(0, NR - 1)], back.at[pl.ds(0, NR - 1)], b_recv).wait()
-
-    @pl.when(jnp.logical_not(same))
-    def _():
-        pltpu.make_async_copy(back.at[pl.ds(0, NR)], back.at[pl.ds(0, NR)], b_recv).wait()
+    lax.fori_loop(1, NB, deliver, 0)
+    back[pl.ds(2 * b, 2)] = fin[pl.ds(2 * b, 2)]
+    pltpu.make_async_copy(back.at[pl.ds(0, NR - 2)], back.at[pl.ds(0, NR - 2)], z_recv).wait()
 
     for i in range(NR):
         back2[i:i + 1, :] = back[i]
@@ -311,15 +328,9 @@
     for way in range(2):
         for step in range(1, NY // 2 + 1):
             ring(way, step, 1, step == NY // 2).wait_send()
-    pltpu.make_async_copy(rows.at[pl.ds(0, NR - 1)], rows.at[pl.ds(0, NR - 1)], a_send).wait()
-
-    @pl.when(same)
-    def _():
-        pltpu.make_async_copy(back.at[pl.ds(0, NR - 1)], back.at[pl.ds(0, NR - 1)], b_send).wait()
-
-    @pl.when(jnp.logical_not(same))
-    def _():
-        pltpu.make_async_copy(back.at[pl.ds(0, NR)], back.at[pl.ds(0, NR)], b_send).wait()
+    pltpu.make_async_copy(red_y.at[pl.ds(0, NY - 1)], red_y.at[pl.ds(0, NY - 1)], y_send).wait()
+    pltpu.make_async_copy(red_x.at[pl.ds(0, NX - 1)], red_x.at[pl.ds(0, NX - 1)], x_send).wait()
+    pltpu.make_async_copy(back.at[pl.ds(0, NR - 2)], back.at[pl.ds(0, NR - 2)], z_send).wait()
 
 
 def per_device(gen_points, bucket_id, ref_points, block_pairs, pair_count):
@@ -331,33 +342,41 @@
             jax.ShapeDtypeStruct((Q, BLK), f32),
             jax.ShapeDtypeStruct((NR, BLK), f32),
         ),
-        in_specs=[vmem] * 4 + [pl.BlockSpec(memory_space=pltpu.SMEM)],
+        in_specs=[pl.BlockSpec(memory_space=pltpu.HBM)] * 4 + [pl.BlockSpec(memory_space=pltpu.SMEM)],
         out_specs=(vmem, vmem),
         scratch_shapes=[
+            pltpu.VMEM((F, GEN), bf16),
+            pltpu.VMEM((Q, BLK), jnp.int32),
+            pltpu.VMEM((F, NR, BLK), bf16),
+            pltpu.VMEM((1, 1, 2, PAIRS), jnp.int32),
+            dma((4,)),
+            pltpu.VMEM((NX, SEND, GEN), bf16),
             pltpu.VMEM((F * NR, BLK), f32),
             pltpu.VMEM((3, NR, BLK), f32),
             pltpu.VMEM((BLK, GEN), bf16),
             pltpu.VMEM((1, GEN), f32),
             pltpu.VMEM((1, GEN), jnp.int32),
             pltpu.VMEM((Q * NB, BLK), bf16),
-            pltpu.VMEM((SEND, BLK), f32),
+            pltpu.VMEM((NX, SEND, BLK), f32),
             pltpu.VMEM((UN, K, BLK), f32),
             pltpu.VMEM((NR, K), f32),
             pltpu.VMEM((NR * BLK, K), bf16),
-            pltpu.VMEM((SEND, BLK), bf16),
+            pltpu.VMEM((NX, SEND, BLK), bf16),
             pltpu.VMEM((NR, SEND, BLK), bf16),
             pltpu.VMEM((K, NX * BLK), bf16),
             pltpu.VMEM((NR * BLK, BLK), f32),
             pltpu.VMEM((NR, 1, BLK), f32),
+            pltpu.VMEM((NY, NR, 1, BLK), f32),
             pltpu.VMEM((NR, 1, BLK), f32),
-            pltpu.VMEM((1, 1, BLK), f32),
+            pltpu.VMEM((NX, NR, 1, BLK), f32),
+            pltpu.VMEM((NR, 1, BLK), f32),
             pltpu.VMEM((NR, 1, BLK), f32),
             pltpu.VMEM((NR, BLK), f32),
             dma((NX,)), dma((NX,)), dma((2, NY // 2)), dma((2, NY // 2)),
-            dma, dma, dma, dma,
+            dma, dma, dma, dma, dma, dma,
         ],
         compiler_params=pltpu.CompilerParams(
-            collective_id=0, has_side_effects=True, vmem_limit_bytes=48 * 2**20
+            collective_id=0, has_side_effects=True, vmem_limit_bytes=56 * 2**20
         ),
         cost_estimate=pl.CostEstimate(
             flops=2 * 4096 * 4096 * 128, bytes_accessed=2**21, transcendentals=0

time: 62.4 us -> 54.3 us (0.87)
  Pallas kernels: 56.1 us -> 50.8 us
  local copies, waits for them, and re-layouts: 4.66 us -> 1.92 us
    pallas_call x1, Pallas kernels: 56.1 us -> 50.8 us  [per_device(): pl.pallas_call(kernel, out_shape=(jax.ShapeDtypeStruct((Q, BLK), f32), ja...]
    unnamed x10 -> x4, local copies, waits for them, and re-layouts: 4.66 us -> 1.92 us
where the time goes in v3:
time: 54.3 us; the launch traced here: 54.1 us
  Pallas kernels  50.8 us (94%)
  local copies, waits for them, and re-layouts  1.92 us (4%)
  between operations  1.29 us (2%)
    pallas_call x1, Pallas kernels, per_device(): pl.pallas_call(kernel, out_shape=(jax.ShapeDtypeStruct((Q, BLK), f32), ja...  50.8 us
    unnamed x4, local copies, waits for them, and re-layouts  1.92 us

profile of v3, /device:TPU:1, one launch (start us, length us, event | category | flops | bytes accessed | tf_op | source)
XLA Modules:
  0.0 54.1 jit_solution(6788531306604941535)
XLA Ops:
  1.3 50.8 %chamfer.1 = (f32[24,128]{1,0:T(8,128)}, f32[32,128]{1,0:T(8,128)}) custom-call(bf16[68,3072]{1,0:T(8,128)(2,1)} %gen_hbm.1, s32[24,128]{1,0:T(8,128)} %bitcast.5, bf16[68,32,128]{2,1,0:T(8,128)(2,1)} %bitcast.4, s32[1,1,2,768]{3,2,1,0:T(2,128)} %pairs_hbm.1, s32[1,1]{1,0:T(1,128)S(6)} %copy.9.count_ref), custom_call_target="tpu_custom_call" | custom-call | flops 4294967296 | bytes 2097152 | tf_op jit(solution)/shard_map/chamfer/pallas_call | solution.py:339
  52.1 0.0 copy-start
  52.1 1.3 %copy.10 = f32[3072]{0:T(1024)} copy(f32[3072]{0:T(1024)} %bitcast.3) | data formatting | bytes 24576
  53.5 0.0 copy-done
  53.5 0.6 %copy.11 = f32[32,128]{1,0:T(8,128)} copy(f32[32,128]{1,0:T(8,128)S(1)} %copy-done) | data formatting | bytes 32768
Async XLA Ops:
  52.1 1.3 %copy-start = (f32[32,128]{1,0:T(8,128)S(1)}, f32[32,128]{1,0:T(8,128)}, u32[]{:S(2)}) copy-start(f32[32,128]{1,0:T(8,128)} %get-tuple-element.9) | copy-start | bytes 49156

commit v4 on v3

--- a/solution.py
+++ b/solution.py
@@ -40,14 +40,35 @@
     gen_ref, bid_ref, rp_ref, pairs_ref, in_sem, picked,
     rpf, rnorm,
     onehot, rank_row, blk_row, ebuf, tmp, xbuf, mrow, rft, gsend, gbuf, gop, colacc,
-    rows, red_y, low_y, red_x, fin, back, back2,
-    s1_send, s1_recv, ring_send, ring_recv, y_send, y_recv, x_send, x_recv, z_send, z_recv,
+    rows, red_y, fin, back, sized, back2,
+    s1_send, s1_recv, ring_send, ring_recv, y_send, y_recv, z_send, z_recv, known,
 ):
     b = lax.axis_index("bucket")
     r = lax.axis_index("ref")
     x, y = r // NY, lax.rem(r, NY)
-    half, turn = lax.rem(y, 2), y // 2
-    mates = [4 * i + lax.rem(turn - b + NB, 4) for i in range(NX)]
+    mates = [4 * i + lax.rem(x - b + NB, 4) for i in range(NX)]
+
+    bar = pltpu.get_barrier_semaphore()
+
+    def at_x(i):
+        return (b, lax.rem(x + i, NX) * NY + y)
+
+    def at_y(i):
+        return (b, x * NY + lax.rem(y + i, NY))
+
+    def at_z(i):
+        return (lax.rem(b + i, NB), r)
+
+    def far_first(j, count):
+        return count // 2 + (j // 2) * (1 - lax.rem(j, 2)) - (j // 2 + 1) * lax.rem(j, 2)
+
+    for peer, count in ((at_z, NB), (at_y, NY), (at_x, NX)):
+        def greet(j, c, peer=peer, count=count):
+            to = peer(far_first(j, count))
+            pl.semaphore_signal(bar, inc=1, device_id=to, device_id_type=MESH)
+            return c
+
+        lax.fori_loop(0, count - 1, greet, 0)
 
     loads = [
         pltpu.make_async_copy(src, dst, in_sem.at[i])
@@ -57,24 +78,6 @@
     ]
     for copy in loads:
         copy.start()
-
-    bar = pltpu.get_barrier_semaphore()
-
-    def at_x(i):
-        return (b, lax.rem(x + i, NX) * NY + y)
-
-    def at_y(i):
-        return (b, x * NY + lax.rem(y + i, NY))
-
-    def at_z(i):
-        return (lax.rem(b + i, NB), r)
-
-    for peer, count in ((at_z, NB), (at_y, NY), (at_x, NX)):
-        def greet(i, c, peer=peer):
-            pl.semaphore_signal(bar, inc=1, device_id=peer(i), device_id_type=MESH)
-            return c
-
-        lax.fori_loop(1, count, greet, 0)
 
     loads[0].wait()
     for q in range(Q):
@@ -95,47 +98,53 @@
         blk_row[:, q * BLK:(q + 1) * BLK] = blk
         onehot[:, q * BLK:(q + 1) * BLK] = (iota((BLK, BLK), 0) == off.astype(jnp.int32)).astype(f32).astype(bf16)
 
+    def first(i, u):
+        slot = (2 * x + u) * NX + b // 4
+        return pltpu.make_async_remote_copy(
+            src_ref=gsend.at[u, i], dst_ref=gbuf.at[slot],
+            send_sem=s1_send.at[u, i], recv_sem=s1_recv.at[u, b // 4],
+            device_id=(mates[i], r), device_id_type=MESH,
+        )
+
     loads[1].wait()
     for i in range(NX):
-        mine = (blk_row[...] == 2 * mates[i] + half).astype(f32).astype(bf16)
-        picked[i, 0:F, :] = gen_ref[...] * mine
         picked[i, F:SEND, :] = jnp.zeros((SEND - F, GEN), bf16)
-    blocks = lax.dot_general(
-        picked[...].reshape(NX * SEND, GEN), onehot[...], (((1,), (1,)), ((), ())),
-        preferred_element_type=f32,
-    )
-    for i in range(NX):
-        block = blocks[i * SEND:(i + 1) * SEND]
-        norm = jnp.sum(block * block, axis=0, keepdims=True)
-        total = jnp.sum(jnp.where(iota((NB, BLK), 0) == mates[i], carry, 0.0), axis=0, keepdims=True)
-        slot_id = iota((1, BLK), 1) + half * BLK
-        norm = jnp.where(slot_id.astype(f32) < total, norm, BIG)
-        tmp[i] = block
-        for j, part in enumerate(three(norm)):
-            tmp[i, F + j:F + j + 1, :] = part
-        tmp[i, F + 3:F + 6, :] = jnp.ones((3, BLK), f32)
-        gsend[i] = tmp[i].astype(bf16)
-
-    pl.semaphore_wait(bar, NB + NX + NY - 3)
-
-    my_slot = y * NX + b // 4
-
-    def first(i):
-        return pltpu.make_async_remote_copy(
-            src_ref=gsend.at[i], dst_ref=gbuf.at[my_slot],
-            send_sem=s1_send.at[i], recv_sem=s1_recv.at[b // 4],
-            device_id=(mates[i], r), device_id_type=MESH,
+    for u in range(2):
+        for i in range(NX):
+            mine = (blk_row[...] == 2 * mates[i] + u).astype(f32).astype(bf16)
+            picked[i, 0:F, :] = gen_ref[...] * mine
+        blocks = lax.dot_general(
+            picked[...].reshape(NX * SEND, GEN), onehot[...], (((1,), (1,)), ((), ())),
+            preferred_element_type=f32,
         )
-
-    for i in range(NX):
-
-        @pl.when(mates[i] != b)
-        def _():
-            first(i).start()
-
-        @pl.when(mates[i] == b)
-        def _():
-            gbuf[my_slot] = gsend[i]
+        for i in range(NX):
+            block = blocks[i * SEND:(i + 1) * SEND]
+            norm = jnp.sum(block * block, axis=0, keepdims=True)
+            total = jnp.sum(
+                jnp.where(iota((NB, BLK), 0) == mates[i], carry, 0.0), axis=0, keepdims=True
+            )
+            slot_id = iota((1, BLK), 1) + u * BLK
+            norm = jnp.where(slot_id.astype(f32) < total, norm, BIG)
+            tmp[i] = block
+            for j, part in enumerate(three(norm)):
+                tmp[i, F + j:F + j + 1, :] = part
+            tmp[i, F + 3:F + 6, :] = jnp.ones((3, BLK), f32)
+            gsend[u, i] = tmp[i].astype(bf16)
+
+        if u == 0:
+            pl.semaphore_wait(bar, NB + NX + NY - 3)
+            for k in range(1, NX):
+                pl.semaphore_signal(known, inc=1, device_id=at_x(k), device_id_type=MESH)
+
+        for i in range(NX):
+
+            @pl.when(mates[i] != b)
+            def _():
+                first(i, u).start()
+
+            @pl.when(mates[i] == b)
+            def _():
+                gbuf[(2 * x + u) * NX + b // 4] = gsend[u, i]
 
     loads[2].wait()
     kid = iota((K, PAIRS), 0) - SEND
@@ -176,7 +185,7 @@
     lax.fori_loop(0, NR // UN // 2, prepare, 0)
 
     def along_y(start, size):
-        for k in range(1, NY):
+        for k in (4, 3, 5, 2, 6, 1, 7):
             pltpu.make_async_remote_copy(
                 src_ref=rows.at[pl.ds(start, size)], dst_ref=red_y.at[y, pl.ds(start, size)],
                 send_sem=y_send, recv_sem=y_recv,
@@ -200,58 +209,59 @@
         for i in range(NX):
             rows[i_step * NX + i] = low[:, i * BLK:(i + 1) * BLK]
 
-    for i in range(NX):
-
-        @pl.when(mates[i] != b)
-        def _():
-            first(i).wait_send()
-            pltpu.make_async_remote_copy(
-                src_ref=gsend.at[i], dst_ref=gbuf.at[y * NX + i],
-                send_sem=s1_send.at[i], recv_sem=s1_recv.at[i],
-                device_id=(mates[i], r), device_id_type=MESH,
-            ).wait_recv()
-
-    def ring(way, step, behind, last):
+    def own_arrived(u):
+        for i in range(NX):
+
+            @pl.when(mates[i] != b)
+            def _():
+                pltpu.make_async_remote_copy(
+                    src_ref=gsend.at[u, i], dst_ref=gbuf.at[(2 * x + u) * NX + i],
+                    send_sem=s1_send.at[u, i], recv_sem=s1_recv.at[u, i],
+                    device_id=(mates[i], r), device_id_type=MESH,
+                ).wait_recv()
+
+    def ring(way, u, step, behind):
         sign = 1 - 2 * way
-        group = lax.rem(y - sign * (step - behind) + 2 * NY, NY)
-        if last:
+        group = 2 * lax.rem(x - sign * (step - behind) + NX, NX) + u
+        if step == 2:
             piece = gbuf.at[pl.ds(group * NX + way * (NX // 2), NX // 2)]
         else:
             piece = gbuf.at[pl.ds(group * NX, NX)]
-        to = lax.rem(y + sign + NY, NY)
         return pltpu.make_async_remote_copy(
             src_ref=piece, dst_ref=piece,
-            send_sem=ring_send.at[way, step - 1], recv_sem=ring_recv.at[way, step - 1],
-            device_id=(b, x * NY + to), device_id_type=MESH,
+            send_sem=ring_send.at[way, u, step - 1], recv_sem=ring_recv.at[way, u, step - 1],
+            device_id=at_x(sign + NX), device_id_type=MESH,
         )
 
-    for way in range(2):
-        ring(way, 1, 1, False).start()
+    def leave(u):
+        own_arrived(u)
+        for way in range(2):
+            ring(way, u, 1, 1).start()
+
+    def pass_on(u):
+        for way in range(2):
+            ring(way, u, 1, 0).wait_recv()
+            ring(way, u, 2, 1).start()
+
+    def last_arrived(u):
+        for way in range(2):
+            ring(way, u, 2, 0).wait_recv()
+
+    leave(0)
     lax.fori_loop(NR // UN // 2, NR // UN, prepare, 0)
+    leave(1)
 
     def group_step(i, c):
-        step = (i + 1) // 2
-        odd = lax.rem(i, 2)
-
-        @pl.when((odd == 1) & (step < NY // 2))
-        def _():
-            for way in range(2):
-                ring(way, step, 0, False).wait_recv()
-
-                @pl.when(step + 1 < NY // 2)
-                def _():
-                    ring(way, step + 1, 1, False).start()
-
-                @pl.when(step + 1 == NY // 2)
-                def _():
-                    ring(way, step + 1, 1, True).start()
-
-        @pl.when(step == NY // 2)
-        def _():
-            for way in range(2):
-                ring(way, step, 0, True).wait_recv()
-
-        compute(i, lax.rem(y + (1 - 2 * odd) * step + NY, NY))
+        for at, what, u in ((2, pass_on, 0), (4, pass_on, 1), (6, last_arrived, 0), (7, last_arrived, 1)):
+
+            @pl.when(i == at)
+            def _():
+                what(u)
+
+        near = (i > 1) & (i < 6)
+        u = jnp.where(near, (i - 2) // 2, lax.rem(i, 2))
+        away = jnp.where(near, 3 - 2 * lax.rem(i, 2), jnp.where(i < 2, 0, 2))
+        compute(i, 2 * lax.rem(x + away, NX) + u)
 
         @pl.when(i == 5)
         def _():
@@ -276,44 +286,42 @@
     lax.fori_loop(0, NR // UN // 2, finish, 0)
 
     pltpu.make_async_copy(red_y.at[pl.ds(0, NY - 1)], red_y.at[pl.ds(0, NY - 1)], y_recv).wait()
-    order = {0: 0, 7: 1, 1: 2, 6: 3, 2: 4, 5: 5, 3: 6, 4: 7}
-    for ahead in range(NY):
-        at = order[ahead] * NX
+    for i in range(2 * NX):
+        at = i * NX
         low = rows[at:at + NX]
         for k in range(1, NY):
-            at = order[(ahead - k) % NY] * NX
             low = jnp.minimum(low, red_y[lax.rem(y + k, NY), at:at + NX])
-        low_y[pl.ds(lax.rem(y + ahead, NY) * NX, NX)] = low
-
-    for k in range(1, NX):
-        pltpu.make_async_remote_copy(
-            src_ref=low_y, dst_ref=red_x.at[x],
-            send_sem=x_send, recv_sem=x_recv, device_id=at_x(k), device_id_type=MESH,
-        ).start()
+        u = (i - 2) // 2 if 1 < i < 6 else i % 2
+        away = 3 - 2 * (i % 2) if 1 < i < 6 else (0 if i < 2 else 2)
+        first_s = lax.rem(x + away - b + NB, 4)
+        for j in range(NX):
+            fin[2 * (4 * j + first_s) + u] = low[j]
+
+    pl.semaphore_wait(known, NX - 1)
+
+    def deliver(j, c):
+        off = far_first(j, NB)
+        s = lax.rem(b + off, NB)
+        for k in (2, 1, 3, 0):
+
+            @pl.when((off != 0) | (k != 0))
+            def _():
+                pltpu.make_async_remote_copy(
+                    src_ref=fin.at[pl.ds(2 * s, 2)], dst_ref=back.at[x, pl.ds(2 * b, 2)],
+                    send_sem=z_send, recv_sem=z_recv,
+                    device_id=(s, lax.rem(x + k, NX) * NY + y), device_id_type=MESH,
+                ).start()
+
+        return c
+
+    lax.fori_loop(0, NB, deliver, 0)
+    back[x, pl.ds(2 * b, 2)] = fin[pl.ds(2 * b, 2)]
     lax.fori_loop(NR // UN // 2, NR // UN, finish, 0)
-    pltpu.make_async_copy(red_x.at[pl.ds(0, NX - 1)], red_x.at[pl.ds(0, NX - 1)], x_recv).wait()
-    for s in range(NB):
-        for h in range(2):
-            slot = (2 * lax.rem(b + s, 4) + h) * NX + s // 4
-            low = low_y[slot]
-            for k in range(1, NX):
-                low = jnp.minimum(low, red_x[lax.rem(x + k, NX), slot])
-            fin[2 * s + h] = low / F
-
-    def deliver(i, c):
-        s = lax.rem(b + i, NB)
-        pltpu.make_async_remote_copy(
-            src_ref=fin.at[pl.ds(2 * s, 2)], dst_ref=back.at[pl.ds(2 * b, 2)],
-            send_sem=z_send, recv_sem=z_recv, device_id=(s, r), device_id_type=MESH,
-        ).start()
-        return c
-
-    lax.fori_loop(1, NB, deliver, 0)
-    back[pl.ds(2 * b, 2)] = fin[pl.ds(2 * b, 2)]
-    pltpu.make_async_copy(back.at[pl.ds(0, NR - 2)], back.at[pl.ds(0, NR - 2)], z_recv).wait()
+    pltpu.make_async_copy(sized, sized, z_recv).wait()
 
     for i in range(NR):
-        back2[i:i + 1, :] = back[i]
+        low = jnp.minimum(jnp.minimum(back[0, i], back[1, i]), jnp.minimum(back[2, i], back[3, i]))
+        back2[i:i + 1, :] = low / F
     hi, mid, lo = three(back2[...])
     parts = jnp.concatenate([hi, mid, lo], axis=0).astype(bf16)
     for q in range(0, Q, 4):
@@ -325,12 +333,18 @@
         for i in range(4):
             gd_ref[q + i:q + i + 1, :] = v[:, i * BLK:(i + 1) * BLK]
 
-    for way in range(2):
-        for step in range(1, NY // 2 + 1):
-            ring(way, step, 1, step == NY // 2).wait_send()
-    pltpu.make_async_copy(red_y.at[pl.ds(0, NY - 1)], red_y.at[pl.ds(0, NY - 1)], y_send).wait()
-    pltpu.make_async_copy(red_x.at[pl.ds(0, NX - 1)], red_x.at[pl.ds(0, NX - 1)], x_send).wait()
-    pltpu.make_async_copy(back.at[pl.ds(0, NR - 2)], back.at[pl.ds(0, NR - 2)], z_send).wait()
+    for u in range(2):
+        for i in range(NX):
+
+            @pl.when(mates[i] != b)
+            def _():
+                first(i, u).wait_send()
+
+        for way in range(2):
+            for step in (1, 2):
+                ring(way, u, step, 1).wait_send()
+    pltpu.make_async_copy(red_y.at[0:NY - 1], red_y.at[0:NY - 1], y_send).wait()
+    pltpu.make_async_copy(sized, sized, z_send).wait()
 
 
 def per_device(gen_points, bucket_id, ref_points, block_pairs, pair_count):
@@ -361,7 +375,7 @@
             pltpu.VMEM((UN, K, BLK), f32),
             pltpu.VMEM((NR, K), f32),
             pltpu.VMEM((NR * BLK, K), bf16),
-            pltpu.VMEM((NX, SEND, BLK), bf16),
+            pltpu.VMEM((2, NX, SEND, BLK), bf16),
             pltpu.VMEM((NR, SEND, BLK), bf16),
             pltpu.VMEM((K, NX * BLK), bf16),
             pltpu.VMEM((NR * BLK, BLK), f32),
@@ -369,11 +383,10 @@
             pltpu.VMEM((NY, NR, 1, BLK), f32),
             pltpu.VMEM((NR, 1, BLK), f32),
             pltpu.VMEM((NX, NR, 1, BLK), f32),
-            pltpu.VMEM((NR, 1, BLK), f32),
-            pltpu.VMEM((NR, 1, BLK), f32),
+            pltpu.VMEM((NX * NR - 2, 1, BLK), f32),
             pltpu.VMEM((NR, BLK), f32),
-            dma((NX,)), dma((NX,)), dma((2, NY // 2)), dma((2, NY // 2)),
-            dma, dma, dma, dma, dma, dma,
+            dma((2, NX)), dma((2, NX)), dma((2, 2, 2)), dma((2, 2, 2)),
+            dma, dma, dma, dma, pltpu.SemaphoreType.REGULAR,
         ],
         compiler_params=pltpu.CompilerParams(
             collective_id=0, has_side_effects=True, vmem_limit_bytes=56 * 2**20

time: 54.3 us -> 48.5 us (0.89)
  Pallas kernels: 50.8 us -> 45.1 us
    pallas_call x1, Pallas kernels: 50.8 us -> 45.1 us  [per_device(): pl.pallas_call(kernel, out_shape=(jax.ShapeDtypeStruct((Q, BLK), f32), ja...]
where the time goes in v4:
time: 48.5 us; the launch traced here: 48.3 us
  Pallas kernels  45.1 us (93%)
  local copies, waits for them, and re-layouts  1.92 us (4%)
  between operations  1.29 us (3%)
    pallas_call x1, Pallas kernels, per_device(): pl.pallas_call(kernel, out_shape=(jax.ShapeDtypeStruct((Q, BLK), f32), ja...  45.1 us
    unnamed x4, local copies, waits for them, and re-layouts  1.92 us

profile of v4, /device:TPU:1, one launch (start us, length us, event | category | flops | bytes accessed | tf_op | source)
XLA Modules:
  0.0 48.3 jit_solution(15968666009706273816)
XLA Ops:
  1.3 45.1 %chamfer.1 = (f32[24,128]{1,0:T(8,128)}, f32[32,128]{1,0:T(8,128)}) custom-call(bf16[68,3072]{1,0:T(8,128)(2,1)} %gen_hbm.1, s32[24,128]{1,0:T(8,128)} %bitcast.5, bf16[68,32,128]{2,1,0:T(8,128)(2,1)} %bitcast.4, s32[1,1,2,768]{3,2,1,0:T(2,128)} %pairs_hbm.1, s32[1,1]{1,0:T(1,128)S(6)} %copy.9.count_ref), custom_call_target="tpu_custom_call" | custom-call | flops 4294967296 | bytes 2097152 | tf_op jit(solution)/shard_map/chamfer/pallas_call | solution.py:353
  46.3 0.0 copy-start
  46.4 1.3 %copy.10 = f32[3072]{0:T(1024)} copy(f32[3072]{0:T(1024)} %bitcast.3) | data formatting | bytes 24576
  47.7 0.0 copy-done
  47.7 0.6 %copy.11 = f32[32,128]{1,0:T(8,128)} copy(f32[32,128]{1,0:T(8,128)S(1)} %copy-done) | data formatting | bytes 32768
Async XLA Ops:
  46.3 1.3 %copy-start = (f32[32,128]{1,0:T(8,128)S(1)}, f32[32,128]{1,0:T(8,128)}, u32[]{:S(2)}) copy-start(f32[32,128]{1,0:T(8,128)} %get-tuple-element.9) | copy-start | bytes 49156

commit v5 on v4

--- a/solution.py
+++ b/solution.py
@@ -46,7 +46,18 @@
     b = lax.axis_index("bucket")
     r = lax.axis_index("ref")
     x, y = r // NY, lax.rem(r, NY)
-    mates = [4 * i + lax.rem(x - b + NB, 4) for i in range(NX)]
+    def quarter(k, c):
+        return 4 * lax.rem(b // 4 + k, 4) + c
+
+    def source(at_x, u, a):
+        c = lax.rem(at_x - b + NB, 4)
+        k = jnp.where(c // 2 - lax.rem(b, 4) // 2 == 1, 3, 1)
+        return quarter(2 * u if a == 0 else (4 - k if u else k), c)
+
+    def target(u, a):
+        c = lax.rem(x - b + NB, 4)
+        k = jnp.where(c // 2 - lax.rem(b, 4) // 2 == -1, 1, 3)
+        return quarter(2 * u if a == 0 else (4 - k if u else k), c)
 
     bar = pltpu.get_barrier_semaphore()
 
@@ -98,12 +109,11 @@
         blk_row[:, q * BLK:(q + 1) * BLK] = blk
         onehot[:, q * BLK:(q + 1) * BLK] = (iota((BLK, BLK), 0) == off.astype(jnp.int32)).astype(f32).astype(bf16)
 
-    def first(i, u):
-        slot = (2 * x + u) * NX + b // 4
+    def first(u, a):
         return pltpu.make_async_remote_copy(
-            src_ref=gsend.at[u, i], dst_ref=gbuf.at[slot],
-            send_sem=s1_send.at[u, i], recv_sem=s1_recv.at[u, b // 4],
-            device_id=(mates[i], r), device_id_type=MESH,
+            src_ref=gsend.at[u, a], dst_ref=gbuf.at[pl.ds((2 * x + u) * NX + 2 * a, 2)],
+            send_sem=s1_send.at[u, a], recv_sem=s1_recv.at[u, a],
+            device_id=(target(u, a), r), device_id_type=MESH,
         )
 
     loads[1].wait()
@@ -111,7 +121,7 @@
         picked[i, F:SEND, :] = jnp.zeros((SEND - F, GEN), bf16)
     for u in range(2):
         for i in range(NX):
-            mine = (blk_row[...] == 2 * mates[i] + u).astype(f32).astype(bf16)
+            mine = (blk_row[...] == 2 * target(u, i // 2) + i % 2).astype(f32).astype(bf16)
             picked[i, 0:F, :] = gen_ref[...] * mine
         blocks = lax.dot_general(
             picked[...].reshape(NX * SEND, GEN), onehot[...], (((1,), (1,)), ((), ())),
@@ -121,34 +131,38 @@
             block = blocks[i * SEND:(i + 1) * SEND]
             norm = jnp.sum(block * block, axis=0, keepdims=True)
             total = jnp.sum(
-                jnp.where(iota((NB, BLK), 0) == mates[i], carry, 0.0), axis=0, keepdims=True
+                jnp.where(iota((NB, BLK), 0) == target(u, i // 2), carry, 0.0), axis=0, keepdims=True
             )
-            slot_id = iota((1, BLK), 1) + u * BLK
+            slot_id = iota((1, BLK), 1) + (i % 2) * BLK
             norm = jnp.where(slot_id.astype(f32) < total, norm, BIG)
             tmp[i] = block
             for j, part in enumerate(three(norm)):
                 tmp[i, F + j:F + j + 1, :] = part
             tmp[i, F + 3:F + 6, :] = jnp.ones((3, BLK), f32)
-            gsend[u, i] = tmp[i].astype(bf16)
+            gsend[u, i // 2, i % 2] = tmp[i].astype(bf16)
 
         if u == 0:
             pl.semaphore_wait(bar, NB + NX + NY - 3)
             for k in range(1, NX):
                 pl.semaphore_signal(known, inc=1, device_id=at_x(k), device_id_type=MESH)
 
-        for i in range(NX):
-
-            @pl.when(mates[i] != b)
-            def _():
-                first(i, u).start()
-
-            @pl.when(mates[i] == b)
-            def _():
-                gbuf[(2 * x + u) * NX + b // 4] = gsend[u, i]
+        for a in range(2):
+
+            @pl.when(target(u, a) != b)
+            def _():
+                first(u, a).start()
+
+            @pl.when(target(u, a) == b)
+            def _():
+                gbuf[pl.ds((2 * x + u) * NX + 2 * a, 2)] = gsend[u, a]
 
     loads[2].wait()
     kid = iota((K, PAIRS), 0) - SEND
-    gid = 8 * (kid & 3) + 2 * (((kid >> 3) - b + NB) & 3) + ((kid >> 2) & 1)
+    c = ((kid >> 3) - b + NB) & 3
+    k = jnp.where((c >> 1) - lax.rem(b, 4) // 2 == 1, 3, 1)
+    far = ((kid >> 2) & 1) == 1
+    k = jnp.where((kid & 2) == 0, jnp.where(far, 2, 0), jnp.where(far, 4 - k, k))
+    gid = 8 * ((b // 4 + k) & 3) + 2 * c + (kid & 1)
     gid = jnp.where((kid >= 0) & (kid < NR), gid, -1)
     live = iota((1, PAIRS), 1) < count_ref[0, 0]
     named = jnp.where(live, pairs_ref[0, 0, 0:1, :], -2)
@@ -210,15 +224,11 @@
             rows[i_step * NX + i] = low[:, i * BLK:(i + 1) * BLK]
 
     def own_arrived(u):
-        for i in range(NX):
-
-            @pl.when(mates[i] != b)
-            def _():
-                pltpu.make_async_remote_copy(
-                    src_ref=gsend.at[u, i], dst_ref=gbuf.at[(2 * x + u) * NX + i],
-                    send_sem=s1_send.at[u, i], recv_sem=s1_recv.at[u, i],
-                    device_id=(mates[i], r), device_id_type=MESH,
-                ).wait_recv()
+        for a in range(2):
+
+            @pl.when(source(x, u, a) != b)
+            def _():
+                first(u, a).wait_recv()
 
     def ring(way, u, step, behind):
         sign = 1 - 2 * way
@@ -249,10 +259,11 @@
 
     leave(0)
     lax.fori_loop(NR // UN // 2, NR // UN, prepare, 0)
-    leave(1)
 
     def group_step(i, c):
-        for at, what, u in ((2, pass_on, 0), (4, pass_on, 1), (6, last_arrived, 0), (7, last_arrived, 1)):
+        for at, what, u in (
+            (1, leave, 1), (2, pass_on, 0), (4, pass_on, 1), (6, last_arrived, 0), (7, last_arrived, 1)
+        ):
 
             @pl.when(i == at)
             def _():
@@ -291,11 +302,9 @@
         low = rows[at:at + NX]
         for k in range(1, NY):
             low = jnp.minimum(low, red_y[lax.rem(y + k, NY), at:at + NX])
-        u = (i - 2) // 2 if 1 < i < 6 else i % 2
-        away = 3 - 2 * (i % 2) if 1 < i < 6 else (0 if i < 2 else 2)
-        first_s = lax.rem(x + away - b + NB, 4)
+        u, away = ((i - 2) // 2, 3 - 2 * (i % 2)) if 1 < i < 6 else (i % 2, 0 if i < 2 else 2)
         for j in range(NX):
-            fin[2 * (4 * j + first_s) + u] = low[j]
+            fin[2 * source(lax.rem(x + away, NX), u, j // 2) + j % 2] = low[j]
 
     pl.semaphore_wait(known, NX - 1)
 
@@ -334,11 +343,11 @@
             gd_ref[q + i:q + i + 1, :] = v[:, i * BLK:(i + 1) * BLK]
 
     for u in range(2):
-        for i in range(NX):
-
-            @pl.when(mates[i] != b)
-            def _():
-                first(i, u).wait_send()
+        for a in range(2):
+
+            @pl.when(target(u, a) != b)
+            def _():
+                first(u, a).wait_send()
 
         for way in range(2):
             for step in (1, 2):
@@ -375,7 +384,7 @@
             pltpu.VMEM((UN, K, BLK), f32),
             pltpu.VMEM((NR, K), f32),
             pltpu.VMEM((NR * BLK, K), bf16),
-            pltpu.VMEM((2, NX, SEND, BLK), bf16),
+            pltpu.VMEM((2, 2, 2, SEND, BLK), bf16),
             pltpu.VMEM((NR, SEND, BLK), bf16),
             pltpu.VMEM((K, NX * BLK), bf16),
             pltpu.VMEM((NR * BLK, BLK), f32),
@@ -385,7 +394,7 @@
             pltpu.VMEM((NX, NR, 1, BLK), f32),
             pltpu.VMEM((NX * NR - 2, 1, BLK), f32),
             pltpu.VMEM((NR, BLK), f32),
-            dma((2, NX)), dma((2, NX)), dma((2, 2, 2)), dma((2, 2, 2)),
+            dma((2, 2)), dma((2, 2)), dma((2, 2, 2)), dma((2, 2, 2)),
             dma, dma, dma, dma, pltpu.SemaphoreType.REGULAR,
         ],
         compiler_params=pltpu.CompilerParams(

time: 48.5 us -> 47.6 us (0.981)
  Pallas kernels: 45.1 us -> 44.2 us
    pallas_call x1, Pallas kernels: 45.1 us -> 44.2 us  [per_device(): pl.pallas_call(kernel, out_shape=(jax.ShapeDtypeStruct((Q, BLK), f32), ja...]
where the time goes in v5:
time: 47.6 us; the launch traced here: 47.4 us
  Pallas kernels  44.2 us (93%)
  local copies, waits for them, and re-layouts  1.92 us (4%)
  between operations  1.29 us (3%)
    pallas_call x1, Pallas kernels, per_device(): pl.pallas_call(kernel, out_shape=(jax.ShapeDtypeStruct((Q, BLK), f32), ja...  44.2 us
    unnamed x4, local copies, waits for them, and re-layouts  1.92 us

profile of v5, /device:TPU:1, one launch (start us, length us, event | category | flops | bytes accessed | tf_op | source)
XLA Modules:
  0.0 47.4 jit_solution(14136392011989588803)
XLA Ops:
  1.3 44.2 %chamfer.1 = (f32[24,128]{1,0:T(8,128)}, f32[32,128]{1,0:T(8,128)}) custom-call(bf16[68,3072]{1,0:T(8,128)(2,1)} %gen_hbm.1, s32[24,128]{1,0:T(8,128)} %bitcast.5, bf16[68,32,128]{2,1,0:T(8,128)(2,1)} %bitcast.4, s32[1,1,2,768]{3,2,1,0:T(2,128)} %pairs_hbm.1, s32[1,1]{1,0:T(1,128)S(6)} %copy.9.count_ref), custom_call_target="tpu_custom_call" | custom-call | flops 4294967296 | bytes 2097152 | tf_op jit(solution)/shard_map/chamfer/pallas_call | solution.py:362
  45.5 0.0 copy-start
  45.5 1.3 %copy.10 = f32[3072]{0:T(1024)} copy(f32[3072]{0:T(1024)} %bitcast.3) | data formatting | bytes 24576
  46.8 0.0 copy-done
  46.8 0.6 %copy.11 = f32[32,128]{1,0:T(8,128)} copy(f32[32,128]{1,0:T(8,128)S(1)} %copy-done) | data formatting | bytes 32768
Async XLA Ops:
  45.5 1.3 %copy-start = (f32[32,128]{1,0:T(8,128)S(1)}, f32[32,128]{1,0:T(8,128)}, u32[]{:S(2)}) copy-start(f32[32,128]{1,0:T(8,128)} %get-tuple-element.9) | copy-start | bytes 49156

commit v6 on v5

--- a/solution.py
+++ b/solution.py
@@ -198,11 +198,11 @@
 
     lax.fori_loop(0, NR // UN // 2, prepare, 0)
 
-    def along_y(start, size):
+    def along_y(part, start, size):
         for k in (4, 3, 5, 2, 6, 1, 7):
             pltpu.make_async_remote_copy(
                 src_ref=rows.at[pl.ds(start, size)], dst_ref=red_y.at[y, pl.ds(start, size)],
-                send_sem=y_send, recv_sem=y_recv,
+                send_sem=y_send, recv_sem=y_recv.at[part],
                 device_id=at_y(k), device_id_type=MESH,
             ).start()
 
@@ -276,11 +276,11 @@
 
         @pl.when(i == 5)
         def _():
-            along_y(0, 6 * NX)
+            along_y(0, 0, 6 * NX)
 
         @pl.when(i == 7)
         def _():
-            along_y(6 * NX, 2 * NX)
+            along_y(1, 6 * NX, 2 * NX)
 
         return c
 
@@ -294,38 +294,42 @@
             rd_ref[pl.ds(k, 1), :] = jnp.min(v, axis=0, keepdims=True) / F
         return c
 
-    lax.fori_loop(0, NR // UN // 2, finish, 0)
-
-    pltpu.make_async_copy(red_y.at[pl.ds(0, NY - 1)], red_y.at[pl.ds(0, NY - 1)], y_recv).wait()
-    for i in range(2 * NX):
-        at = i * NX
-        low = rows[at:at + NX]
-        for k in range(1, NY):
-            low = jnp.minimum(low, red_y[lax.rem(y + k, NY), at:at + NX])
-        u, away = ((i - 2) // 2, 3 - 2 * (i % 2)) if 1 < i < 6 else (i % 2, 0 if i < 2 else 2)
-        for j in range(NX):
-            fin[2 * source(lax.rem(x + away, NX), u, j // 2) + j % 2] = low[j]
+    def reduce_y(part, groups):
+        size = len(groups) * NX
+        whole = red_y.at[0:NY - 1, 0:size]
+        pltpu.make_async_copy(whole, whole, y_recv.at[part]).wait()
+        for i in groups:
+            at = i * NX
+            low = rows[at:at + NX]
+            for k in range(1, NY):
+                low = jnp.minimum(low, red_y[lax.rem(y + k, NY), at:at + NX])
+            u, away = ((i - 2) // 2, 3 - 2 * (i % 2)) if 1 < i < 6 else (i % 2, 0 if i < 2 else 2)
+            for j in range(NX):
+                fin[2 * source(lax.rem(x + away, NX), u, j // 2) + j % 2] = low[j]
+
+    def deliver(aways):
+        for k in (2, 1, 3, 0):
+            for u in (1, 0):
+                for a in range(2):
+                    for away in aways:
+                        s = source(lax.rem(x + away, NX), u, a)
+
+                        @pl.when((s != b) | (k != 0))
+                        def _():
+                            pltpu.make_async_remote_copy(
+                                src_ref=fin.at[pl.ds(2 * s, 2)], dst_ref=back.at[x, pl.ds(2 * b, 2)],
+                                send_sem=z_send, recv_sem=z_recv,
+                                device_id=(s, lax.rem(x + k, NX) * NY + y), device_id_type=MESH,
+                            ).start()
 
     pl.semaphore_wait(known, NX - 1)
-
-    def deliver(j, c):
-        off = far_first(j, NB)
-        s = lax.rem(b + off, NB)
-        for k in (2, 1, 3, 0):
-
-            @pl.when((off != 0) | (k != 0))
-            def _():
-                pltpu.make_async_remote_copy(
-                    src_ref=fin.at[pl.ds(2 * s, 2)], dst_ref=back.at[x, pl.ds(2 * b, 2)],
-                    send_sem=z_send, recv_sem=z_recv,
-                    device_id=(s, lax.rem(x + k, NX) * NY + y), device_id_type=MESH,
-                ).start()
-
-        return c
-
-    lax.fori_loop(0, NB, deliver, 0)
+    reduce_y(0, range(6))
+    deliver((0, 3, 1))
+    lax.fori_loop(0, NR // UN // 4, finish, 0)
+    reduce_y(1, (6, 7))
+    deliver((2,))
     back[x, pl.ds(2 * b, 2)] = fin[pl.ds(2 * b, 2)]
-    lax.fori_loop(NR // UN // 2, NR // UN, finish, 0)
+    lax.fori_loop(NR // UN // 4, NR // UN, finish, 0)
     pltpu.make_async_copy(sized, sized, z_recv).wait()
 
     for i in range(NR):
@@ -395,7 +399,7 @@
             pltpu.VMEM((NX * NR - 2, 1, BLK), f32),
             pltpu.VMEM((NR, BLK), f32),
             dma((2, 2)), dma((2, 2)), dma((2, 2, 2)), dma((2, 2, 2)),
-            dma, dma, dma, dma, pltpu.SemaphoreType.REGULAR,
+            dma, dma((2,)), dma, dma, pltpu.SemaphoreType.REGULAR,
         ],
         compiler_params=pltpu.CompilerParams(
             collective_id=0, has_side_effects=True, vmem_limit_bytes=56 * 2**20

time: 47.6 us -> 46.6 us (0.979)
  Pallas kernels: 44.2 us -> 43.2 us
    pallas_call x1, Pallas kernels: 44.2 us -> 43.2 us  [per_device(): pl.pallas_call(kernel, out_shape=(jax.ShapeDtypeStruct((Q, BLK), f32), ja...]
where the time goes in v6:
time: 46.6 us; the launch traced here: 46.4 us
  Pallas kernels  43.2 us (93%)
  local copies, waits for them, and re-layouts  1.92 us (4%)
  between operations  1.29 us (3%)
    pallas_call x1, Pallas kernels, per_device(): pl.pallas_call(kernel, out_shape=(jax.ShapeDtypeStruct((Q, BLK), f32), ja...  43.2 us
    unnamed x4, local copies, waits for them, and re-layouts  1.92 us

profile of v6, /device:TPU:1, one launch (start us, length us, event | category | flops | bytes accessed | tf_op | source)
XLA Modules:
  0.0 46.4 jit_solution(2218853343986800501)
XLA Ops:
  1.3 43.2 %chamfer.1 = (f32[24,128]{1,0:T(8,128)}, f32[32,128]{1,0:T(8,128)}) custom-call(bf16[68,3072]{1,0:T(8,128)(2,1)} %gen_hbm.1, s32[24,128]{1,0:T(8,128)} %bitcast.5, bf16[68,32,128]{2,1,0:T(8,128)(2,1)} %bitcast.4, s32[1,1,2,768]{3,2,1,0:T(2,128)} %pairs_hbm.1, s32[1,1]{1,0:T(1,128)S(6)} %copy.9.count_ref), custom_call_target="tpu_custom_call" | custom-call | flops 4294967296 | bytes 2097152 | tf_op jit(solution)/shard_map/chamfer/pallas_call | solution.py:366
  44.5 0.0 copy-start
  44.5 1.3 %copy.10 = f32[3072]{0:T(1024)} copy(f32[3072]{0:T(1024)} %bitcast.3) | data formatting | bytes 24576
  45.8 0.0 copy-done
  45.8 0.6 %copy.11 = f32[32,128]{1,0:T(8,128)} copy(f32[32,128]{1,0:T(8,128)S(1)} %copy-done) | data formatting | bytes 32768
Async XLA Ops:
  44.5 1.3 %copy-start = (f32[32,128]{1,0:T(8,128)S(1)}, f32[32,128]{1,0:T(8,128)}, u32[]{:S(2)}) copy-start(f32[32,128]{1,0:T(8,128)} %get-tuple-element.9) | copy-start | bytes 49156
